TPU v7x, 32 devices: a whole 2x2x4 slice. The times are simulated.
32 devices in a mesh: dp: 4 (over y, x), tensor: 8 (over z, core).
Axes of the slice: x: 2, y: 2, z: 4, core: 2. Of those that a mesh axis runs over, the one named last changes fastest.
Arguments:
- tokens: bfloat16 [512, 8192], P('tensor', 'dp'), may hold values from -6 to 6
- cotangent: bfloat16 [512, 8192], P('tensor', 'dp'), may hold values from -0.625 to 0.625
- gate_weight: bfloat16 [8192, 14336], P('dp', 'tensor'), may hold values from -0.0625 to 0.0625
- up_weight: bfloat16 [8192, 14336], P('dp', 'tensor'), may hold values from -0.0625 to 0.0625
- down_weight: bfloat16 [14336, 8192], P('tensor', 'dp'), may hold values from -0.046875 to 0.046875
- gate_in: bfloat16 [16, 8192, 16], P(None, 'dp'), may hold values from -0.0625 to 0.0625
- up_in: bfloat16 [16, 8192, 16], P(None, 'dp'), may hold values from -0.0625 to 0.0625
- down_out: bfloat16 [16, 16, 8192], P(None, None, 'dp'), may hold values from -1.5 to 1.5
- gate_out: bfloat16 [16, 16, 14336], P(None, None, 'tensor'), may hold values from -1.5 to 1.5
- up_out: bfloat16 [16, 16, 14336], P(None, None, 'tensor'), may hold values from -1.5 to 1.5
- down_in: bfloat16 [16, 14336, 16], P(None, 'tensor'), may hold values from -0.046875 to 0.046875
- tenants: int32 [8], replicated, may hold values from 0 to 15
- owners: int32 [16], replicated, may hold values from 0 to 15, each once
Outputs:
- mixed: bfloat16 [512, 8192], P('tensor', 'dp')
- grad_gate_in: float32 [16, 8192, 16], P('tensor', 'dp')
- grad_up_in: float32 [16, 8192, 16], P('tensor', 'dp')
- grad_down_out: float32 [16, 16, 8192], P('tensor', None, 'dp')
- grad_gate_out: float32 [16, 16, 14336], P('dp', None, 'tensor')
- grad_up_out: float32 [16, 16, 14336], P('dp', None, 'tensor')
- grad_down_in: float32 [16, 14336, 16], P('dp', 'tensor')
Inputs may be any that keep to these rules, and one draw needn't show every extreme that they name: `tenants`: tenant numbers lie in 0 to 15; a tenant may own no block. `owners`: every owner slot is given to exactly one tenant.
All inputs are finite; a program needn't handle non-finite values.
Results may differ from a plain program's by a relative error of at most 0.029.
Values may be sent and summed in bfloat16 or wider, within the bound.
A program may use at most 128 MiB of HBM per device.

v0:
```python
import jax
import jax.numpy as jnp
from jax import lax
from jax.sharding import PartitionSpec as P

BLOCK = 64


adapter_scale = 0.5


def shards(
    tokens,
    cotangent,
    gate_weight,
    up_weight,
    down_weight,
    gate_in,
    up_in,
    down_out,
    gate_out,
    up_out,
    down_in,
    tenants,
    owners,
):
    highest = lax.Precision.HIGHEST
    dp_count = lax.axis_size("dp")
    tensor_count = lax.axis_size("tensor")
    dp_index = lax.axis_index("dp")
    tensor_index = lax.axis_index("tensor")
    rows_in = tokens.shape[0]
    feat_here = tokens.shape[1]
    width_here = gate_weight.shape[1]
    rank_width = gate_in.shape[2]
    every_token_row = rows_in * tensor_count
    group_rows = every_token_row // dp_count
    blocks_all = tenants.shape[0]
    blocks_group = group_rows // BLOCK
    blocks_in = rows_in // BLOCK
    tenant_count = owners.shape[0]
    slots_here = tenant_count // dp_count
    tenants_here = tenant_count // tensor_count
    group_tenants = lax.dynamic_slice_in_dim(tenants, dp_index * blocks_group, blocks_group)
    input_tenants = lax.dynamic_slice_in_dim(tenants, tensor_index * blocks_in, blocks_in)
    contract_rows = (((0,), (0,)), ((), ()))
    token_tenants = jnp.broadcast_to(tenants[:, None], (blocks_all, BLOCK)).reshape(every_token_row)
    held_tenants = tensor_index * tenants_here + jnp.arange(tenants_here, dtype=jnp.int32)
    token_onehot = (token_tenants[:, None] == held_tenants[None, :]).astype(jnp.bfloat16)
    all_inputs = lax.all_gather(tokens, "tensor", axis=0, tiled=True)
    gate_part = jnp.dot(all_inputs, gate_weight, preferred_element_type=jnp.float32)
    up_part = jnp.dot(all_inputs, up_weight, preferred_element_type=jnp.float32)
    input_blocks = all_inputs.reshape(blocks_all, BLOCK, feat_here)
    gate_rank_part = jnp.einsum(
        "btk,bkr->btr", input_blocks, gate_in[tenants], preferred_element_type=jnp.float32
    ).reshape(every_token_row, rank_width)
    up_rank_part = jnp.einsum(
        "btk,bkr->btr", input_blocks, up_in[tenants], preferred_element_type=jnp.float32
    ).reshape(every_token_row, rank_width)
    gate_total_sum, up_total_sum, gate_rank, up_rank = (
        lax.psum_scatter(
            gate_part.astype(jnp.bfloat16), "dp", scatter_dimension=0, tiled=True
        ).astype(jnp.float32),
        lax.psum_scatter(
            up_part.astype(jnp.bfloat16), "dp", scatter_dimension=0, tiled=True
        ).astype(jnp.float32),
        lax.psum_scatter(
            gate_rank_part.astype(jnp.bfloat16), "dp", scatter_dimension=0, tiled=True
        ).astype(jnp.float32),
        lax.psum_scatter(
            up_rank_part.astype(jnp.bfloat16), "dp", scatter_dimension=0, tiled=True
        ).astype(jnp.float32),
    )
    gate_rank_second = gate_rank.astype(jnp.bfloat16).reshape(blocks_group, BLOCK, rank_width)
    up_rank_second = up_rank.astype(jnp.bfloat16).reshape(blocks_group, BLOCK, rank_width)
    gate_raise = gate_out[group_tenants]
    up_raise = up_out[group_tenants]
    gate_complete = gate_total_sum + adapter_scale * jnp.einsum(
        "uim,umn->uin", gate_rank_second, gate_raise, preferred_element_type=jnp.float32
    ).reshape(group_rows, width_here)
    up_complete = up_total_sum + adapter_scale * jnp.einsum(
        "uim,umn->uin", up_rank_second, up_raise, preferred_element_type=jnp.float32
    ).reshape(group_rows, width_here)
    hidden = (jax.nn.silu(gate_complete) * up_complete).astype(jnp.bfloat16)
    all_hidden = lax.all_gather(hidden, "dp", axis=0, tiled=True)
    out_part = jnp.dot(all_hidden, down_weight, preferred_element_type=jnp.float32)
    down_rank_part = jnp.einsum(
        "btf,bfr->btr",
        all_hidden.reshape(blocks_all, BLOCK, width_here),
        down_in[tenants],
        preferred_element_type=jnp.float32,
    ).reshape(every_token_row, rank_width)
    out_sum, down_rank = (
        lax.psum_scatter(
            out_part.astype(jnp.bfloat16), "tensor", scatter_dimension=0, tiled=True
        ).astype(jnp.float32),
        lax.psum_scatter(
            down_rank_part.astype(jnp.bfloat16), "tensor", scatter_dimension=0, tiled=True
        ).astype(jnp.float32),
    )
    down_rank_flat = down_rank.astype(jnp.bfloat16)
    down_rank_second = down_rank_flat.reshape(blocks_in, BLOCK, rank_width)
    down_raise = down_out[input_tenants]
    mixed = (
        out_sum
        + adapter_scale
        * jnp.einsum(
            "vmn,vnx->vmx", down_rank_second, down_raise, preferred_element_type=jnp.float32
        ).reshape(rows_in, feat_here)
    ).astype(jnp.bfloat16)
    cotangent_block_list = cotangent.reshape(blocks_in, BLOCK, feat_here)
    down_backward_piece = adapter_scale * jnp.einsum(
        "env,ejv->enj", cotangent_block_list, down_raise, preferred_element_type=jnp.float32
    )
    down_backward = lax.psum(down_backward_piece, "dp").astype(jnp.bfloat16)
    tenant_ids = jnp.arange(tenant_count, dtype=jnp.int32)
    input_onehot = (tenant_ids[:, None] == input_tenants[None, :]).astype(jnp.float32)
    raise_gradient_block_list = adapter_scale * jnp.einsum(
        "jpy,jpz->jyz", down_rank_second, cotangent_block_list, preferred_element_type=jnp.float32
    )
    lift_grad_part = jnp.einsum(
        "eb,brd->erd", input_onehot, raise_gradient_block_list, precision=highest
    )
    grad_down_out = lax.psum_scatter(
        lift_grad_part.astype(jnp.bfloat16), "tensor", scatter_dimension=0, tiled=True
    ).astype(jnp.float32)
    all_cot, all_down_back = (
        lax.all_gather(cotangent, "tensor", axis=0, tiled=True),
        lax.all_gather(down_backward.reshape(rows_in, rank_width), "tensor", axis=0, tiled=True),
    )
    hidden_grad_part = lax.dot_general(
        all_cot, down_weight, (((1,), (1,)), ((), ())), preferred_element_type=jnp.float32
    )
    hidden_grad_sum = lax.psum_scatter(
        hidden_grad_part.astype(jnp.bfloat16), "dp", scatter_dimension=0, tiled=True
    ).astype(jnp.float32)
    group_down_back = lax.dynamic_slice_in_dim(
        all_down_back, dp_index * group_rows, group_rows
    ).reshape(blocks_group, BLOCK, rank_width)
    down_drop = down_in[group_tenants]
    hidden_grad = hidden_grad_sum + jnp.einsum(
        "btr,bfr->btf", group_down_back, down_drop, preferred_element_type=jnp.float32
    ).reshape(group_rows, width_here)
    sig = jax.nn.sigmoid(gate_complete)
    up_gradient = (
        (hidden_grad * gate_complete * sig)
        .astype(jnp.bfloat16)
        .reshape(blocks_group, BLOCK, width_here)
    )
    gate_gradient = (
        (hidden_grad * up_complete * sig * (1.0 + gate_complete * (1.0 - sig)))
        .astype(jnp.bfloat16)
        .reshape(blocks_group, BLOCK, width_here)
    )
    gate_backward_piece = adapter_scale * jnp.einsum(
        "yae,yve->yav", gate_gradient, gate_raise, preferred_element_type=jnp.float32
    )
    up_backward_piece = adapter_scale * jnp.einsum(
        "yae,yve->yav", up_gradient, up_raise, preferred_element_type=jnp.float32
    )
    gate_backward, up_backward = lax.psum((gate_backward_piece, up_backward_piece), "tensor")
    gate_raise_block_list = adapter_scale * jnp.einsum(
        "yap,yau->ypu", gate_rank_second, gate_gradient, preferred_element_type=jnp.float32
    )
    up_raise_block_list = adapter_scale * jnp.einsum(
        "yap,yau->ypu", up_rank_second, up_gradient, preferred_element_type=jnp.float32
    )
    own_slots = dp_index * slots_here + jnp.arange(slots_here, dtype=jnp.int32)
    group_onehot = (tenant_ids[:, None] == owners[group_tenants][None, :]).astype(jnp.float32)
    gate_lift_part = jnp.einsum(
        "sb,brf->srf", group_onehot, gate_raise_block_list, precision=highest
    )
    up_lift_part = jnp.einsum("sb,brf->srf", group_onehot, up_raise_block_list, precision=highest)
    grad_gate_out, grad_up_out = (
        lax.psum_scatter(
            gate_lift_part.astype(jnp.bfloat16), "dp", scatter_dimension=0, tiled=True
        ).astype(jnp.float32),
        lax.psum_scatter(
            up_lift_part.astype(jnp.bfloat16), "dp", scatter_dimension=0, tiled=True
        ).astype(jnp.float32),
    )
    all_gate_back, all_up_back = (
        lax.all_gather(
            gate_backward.astype(jnp.bfloat16).reshape(group_rows, rank_width),
            "dp",
            axis=0,
            tiled=True,
        ),
        lax.all_gather(
            up_backward.astype(jnp.bfloat16).reshape(group_rows, rank_width),
            "dp",
            axis=0,
            tiled=True,
        ),
    )
    gate_weighted = (token_onehot[:, :, None] * all_gate_back[:, None, :]).reshape(
        every_token_row, tenants_here * rank_width
    )
    up_weighted = (token_onehot[:, :, None] * all_up_back[:, None, :]).reshape(
        every_token_row, tenants_here * rank_width
    )
    grad_gate_in = (
        lax.dot_general(
            all_inputs, gate_weighted, contract_rows, preferred_element_type=jnp.float32
        )
        .reshape(feat_here, tenants_here, rank_width)
        .transpose(1, 0, 2)
    )
    grad_up_in = (
        lax.dot_general(all_inputs, up_weighted, contract_rows, preferred_element_type=jnp.float32)
        .reshape(feat_here, tenants_here, rank_width)
        .transpose(1, 0, 2)
    )
    token_slots = owners[token_tenants]
    slot_onehot = (token_slots[:, None] == own_slots[None, :]).astype(jnp.bfloat16)
    drop_weighted = (slot_onehot[:, :, None] * all_down_back[:, None, :]).reshape(
        every_token_row, slots_here * rank_width
    )
    grad_down_in = (
        lax.dot_general(
            all_hidden, drop_weighted, contract_rows, preferred_element_type=jnp.float32
        )
        .reshape(width_here, slots_here, rank_width)
        .transpose(1, 0, 2)
    )
    return (
        mixed,
        grad_gate_in,
        grad_up_in,
        grad_down_out,
        grad_gate_out,
        grad_up_out,
        grad_down_in,
    )


def solution(mesh):
    in_specs = (
        P("tensor", "dp"),
        P("tensor", "dp"),
        P("dp", "tensor"),
        P("dp", "tensor"),
        P("tensor", "dp"),
        P(None, "dp", None),
        P(None, "dp", None),
        P(None, None, "dp"),
        P(None, None, "tensor"),
        P(None, None, "tensor"),
        P(None, "tensor", None),
        P(),
        P(),
    )
    out_specs = (
        P("tensor", "dp"),
        P("tensor", "dp", None),
        P("tensor", "dp", None),
        P("tensor", None, "dp"),
        P("dp", None, "tensor"),
        P("dp", None, "tensor"),
        P("dp", "tensor", None),
    )
    return jax.shard_map(shards, mesh=mesh, in_specs=in_specs, out_specs=out_specs, check_vma=False)
```

profile of v0, /device:TPU:0, one launch (start us, length us, event | category | flops | bytes accessed | tf_op | source)
XLA Modules:
  0.0 441.4 jit_solution(2783669415510616488)
XLA Ops:
  11.2 30.3 %all-gather.5.cloned.1.call-done = bf16[512,2048]{1,0:T(8,128)(2,1)} async-done(((bf16[64,2048]{1,0:T(8,128)(2,1)}), bf16[512,2048]{1,0:T(8,128)(2,1)}) %all-gather.5.cloned.1.call-update) | async-done | bytes 2097168 | tf_op jit(solution)/shard_map/all_gather | solution.py:50
  41.5 2.2 fusion.3
  44.5 2.3 fusion.4
  47.7 24.0 %all-gather.9.cloned.1.call-done = bf16[512,2048]{1,0:T(8,128)(2,1)} async-done(((bf16[64,2048]{1,0:T(8,128)(2,1)}), bf16[512,2048]{1,0:T(8,128)(2,1)}) %all-gather.9.cloned.1.call-update) | async-done | bytes 2097168 | tf_op jit(solution)/shard_map/all_gather | solution.py:128
  71.7 9.0 %convolution_convert_fusion = bf16[512,1792]{1,0:T(8,128)(2,1)} fusion(bf16[512,2048]{1,0:T(8,128)(2,1)} %all-gather.9.cloned.1.call-done, bf16[1792,2048]{1,0:T(8,128)(2,1)} %param.17), kind=kOutput, calls=%fused_computation.7 | convolution fusion | flops 3759013888 | bytes 11272192 | tf_op jit(solution)/shard_map/dot_general | solution.py:131
  80.7 8.2 %convolution_convert_fusion.3 = bf16[512,1792]{1,0:T(8,128)(2,1)} fusion(bf16[512,2048]{1,0:T(8,128)(2,1)S(1)} %copy-done.2, bf16[2048,1792]{1,0:T(8,128)(2,1)} %param.15), kind=kOutput, calls=%fused_computation.10 | convolution fusion | flops 3759013888 | bytes 11272192 | tf_op jit(solution)/shard_map/dot_general | solution.py:51
  89.0 8.2 %convolution_convert_fusion.2 = bf16[512,1792]{1,0:T(8,128)(2,1)} fusion(bf16[512,2048]{1,0:T(8,128)(2,1)S(1)} %copy-done.2, bf16[2048,1792]{1,0:T(8,128)(2,1)} %param.16), kind=kOutput, calls=%fused_computation.9 | convolution fusion | flops 3759013888 | bytes 11272192 | tf_op jit(solution)/shard_map/dot_general | solution.py:52
  100.8 10.1 %psum.21 = bf16[1,64,16]{1,2,0:T(8,128)(2,1)S(1)} all-reduce(f32[1,64,16]{1,2,0:T(8,128)S(1)} %fusion.5), channel_id=1, replica_groups=mesh['dp'=4,'tensor'=8] {'dp'}, use_global_device_ids=true, to_apply=%region_7.8 | all-reduce | flops 1024 | bytes 6144 | tf_op jit(solution)/shard_map/psum | solution.py:115
  111.0 14.2 %all-gather = bf16[1,512,16]{2,0,1:T(2,128)(2,1)S(1)} all-gather(bf16[1,64,16]{2,0,1:T(2,128)(2,1)S(1)} %copy.54), channel_id=2, replica_groups=mesh['dp'=4,'tensor'=8] {'tensor'}, dimensions={1}, use_global_device_ids=true | all-gather | bytes 18432 | tf_op jit(solution)/shard_map/all_gather | solution.py:129
  126.8 1.7 gather_fusion.1
  128.6 1.8 gather_fusion.3
  130.7 2.0 convolution_multiply_fusion.1
  132.7 2.0 convolution_multiply_fusion
  134.7 26.9 %reduce-scatter.23.cloned.1.call-done = bf16[128,1792]{1,0:T(8,128)(2,1)} async-done(((bf16[512,1792]{1,0:T(8,128)(2,1)}), bf16[128,1792]{1,0:T(8,128)(2,1)}) %reduce-scatter.23.cloned.1.call-update) | async-done | bytes 458768 | tf_op jit(solution)/shard_map/reduce_scatter | solution.py:134
  161.6 35.9 %reduce-scatter.17.cloned.1.call-done = bf16[128,1792]{1,0:T(8,128)(2,1)} async-done(((bf16[512,1792]{1,0:T(8,128)(2,1)}), bf16[128,1792]{1,0:T(8,128)(2,1)}) %reduce-scatter.17.cloned.1.call-update) | async-done | bytes 458768 | tf_op jit(solution)/shard_map/reduce_scatter | solution.py:61
  197.6 36.1 %reduce-scatter.19.cloned.1.call-done = bf16[128,1792]{1,0:T(8,128)(2,1)} async-done(((bf16[512,1792]{1,0:T(8,128)(2,1)}), bf16[128,1792]{1,0:T(8,128)(2,1)}) %reduce-scatter.19.cloned.1.call-update) | async-done | bytes 458768 | tf_op jit(solution)/shard_map/reduce_scatter | solution.py:64
  233.6 3.4 multiply_convert_fusion.1
  239.7 30.7 %all-gather.7.cloned.1.call-done = bf16[512,1792]{1,0:T(8,128)(2,1)} async-done(((bf16[128,1792]{1,0:T(8,128)(2,1)}), bf16[512,1792]{1,0:T(8,128)(2,1)}) %all-gather.7.cloned.1.call-update) | async-done | bytes 1835024 | tf_op jit(solution)/shard_map/all_gather | solution.py:85
  270.4 2.1 convolution_convert_fusion.6
  279.3 24.2 %reduce-scatter.35.cloned.1.call-done = bf16[64,16]{1,0:T(8,128)(2,1)} async-done(((bf16[512,16]{1,0:T(8,128)(2,1)}), bf16[64,16]{1,0:T(8,128)(2,1)}) %reduce-scatter.35.cloned.1.call-update) | async-done | bytes 2064
  305.7 8.3 %convolution_convert_fusion.1 = bf16[512,2048]{1,0:T(8,128)(2,1)} fusion(bf16[512,1792]{1,0:T(8,128)(2,1)S(1)} %copy-done.9, bf16[1792,2048]{1,0:T(8,128)(2,1)} %param.17), kind=kOutput, calls=%fused_computation.8 | convolution fusion | flops 3759144960 | bytes 11272192 | tf_op jit(solution)/shard_map/dot_general | solution.py:86
  315.1 4.4 %compare_select_fusion.1 = (s32[512,1]{0,1:T(1,128)S(1)}, s32[512,1]{0,1:T(1,128)S(1)}) fusion(s32[]{:T(128)} %bitcast.33, s32[]{:T(128)} %bitcast.34, s32[]{:T(128)} %bitcast.35, s32[]{:T(128)} %bitcast.36, s32[]{:T(128)} %bitcast.37, s32[]{:T(128)} %bitcast.39, s32[]{:T(128)} %bitcast.38, s32[512,1]{0,1:T(1,128)S(1)} %reshape.232), kind=kLoop, calls=%fused_computation.64 | loop fusion | flops 7680 | bytes 6172 | tf_op jit(solution)/shard_map/gather | solution.py:214
  319.6 5.6 %select_select_fusion = s32[512]{0:T(512)S(1)} fusion(pred[512]{0:T(512)(128)(4,1)S(1)} %get-tuple-element.40, pred[512]{0:T(512)(128)(4,1)S(1)} %get-tuple-element.39, pred[512]{0:T(512)(128)(4,1)S(1)} %get-tuple-element.38, pred[512]{0:T(512)(128)(4,1)S(1)} %get-tuple-element.37, pred[512]{0:T(512)(128)(4,1)S(1)} %get-tuple-element.36, ...), kind=kLoop, calls=%fused_computation.76 | loop fusion | flops 4608 | bytes 8740 | tf_op jit(solution)/shard_map/gather | solution.py:214
  327.9 26.0 %all-reduce = (bf16[2,64,16]{1,2,0:T(8,128)(2,1)S(1)}, bf16[2,64,16]{1,2,0:T(8,128)(2,1)S(1)}) all-reduce(f32[2,64,16]{1,2,0:T(8,128)S(1)} %convolution_multiply_fusion.7, f32[2,64,16]{1,2,0:T(8,128)S(1)} %convolution_multiply_fusion.6), channel_id=1, replica_groups=mesh['dp'=4,'tensor'=8] {'tensor'}, use_global_device_ids=true, to_apply=%region_8.9 | all-reduce | flops 4096 | bytes 24576 | tf_op jit(solution)/shard_map/psum | solution.py:161
  354.1 8.1 %all_gather.23 = bf16[512,16]{0,1:T(8,128)(2,1)S(1)} all-gather(bf16[128,16]{0,1:T(8,128)(2,1)S(1)} %reshape.230), channel_id=1, replica_groups=mesh['dp'=4,'tensor'=8] {'dp'}, dimensions={0}, use_global_device_ids=true | all-gather | bytes 20480 | tf_op jit(solution)/shard_map/all_gather | solution.py:189
  362.2 8.0 %all_gather.22 = bf16[512,16]{0,1:T(8,128)(2,1)S(1)} all-gather(bf16[128,16]{0,1:T(8,128)(2,1)S(1)} %reshape.227), channel_id=1, replica_groups=mesh['dp'=4,'tensor'=8] {'dp'}, dimensions={0}, use_global_device_ids=true | all-gather | bytes 20480 | tf_op jit(solution)/shard_map/all_gather | solution.py:183
  372.6 1.7 convert_element_type.136
  374.3 1.7 convert_element_type.138
  376.1 2.7 convolution_bitcast_fusion
  378.8 17.8 %reduce-scatter.25.cloned.1.call-done = bf16[2,16,2048]{2,1,0:T(8,128)(2,1)} async-done(((bf16[16,16,2048]{2,1,0:T(8,128)(2,1)}), bf16[2,16,2048]{2,1,0:T(8,128)(2,1)}) %reduce-scatter.25.cloned.1.call-update) | async-done | bytes 131088 | tf_op jit(solution)/shard_map/reduce_scatter | solution.py:124
  398.2 34.8 %reduce-scatter.21.cloned.1.call-done = bf16[64,2048]{1,0:T(8,128)(2,1)} async-done(((bf16[512,2048]{1,0:T(8,128)(2,1)}), bf16[64,2048]{1,0:T(8,128)(2,1)}) %reduce-scatter.21.cloned.1.call-update) | async-done | bytes 262160 | tf_op jit(solution)/shard_map/reduce_scatter | solution.py:94
  433.0 1.9 fusion.1
  (112 shorter events, 29.1 us)
Async XLA Ops:
  7.2 2.2 copy-start
  7.2 34.3 %all-gather.5.cloned.1.call-start = ((), (), s32[]{:S(2)}) async-start(), calls=%async_computation.10 | async-start | bytes 2359296 | tf_op jit(solution)/shard_map/all_gather | solution.py:50
  7.9 63.8 %all-gather.9.cloned.1.call-start = ((), (), s32[]{:S(2)}) async-start(), calls=%async_computation.15 | async-start | bytes 2359296 | tf_op jit(solution)/shard_map/all_gather | solution.py:128
  8.7 122.0 %reduce-scatter.31.cloned.1.call-start = ((), (), s32[]{:S(2)}) async-start(), calls=%async_computation.20 | async-start | bytes 163840
  9.4 1.2 copy-start.5
  44.5 88.2 %reduce-scatter.33.cloned.1.call-start = ((), (), s32[]{:S(2)}) async-start(), calls=%async_computation.21 | async-start | bytes 163840
  47.6 33.1 %copy-start.2 = (bf16[512,2048]{1,0:T(8,128)(2,1)S(1)}, bf16[512,2048]{1,0:T(8,128)(2,1)}, u32[]{:S(2)}) copy-start(bf16[512,2048]{1,0:T(8,128)(2,1)} %all-gather.5.cloned.1.call-done) | copy-start | bytes 6291460
  47.6 114.0 %reduce-scatter.23.cloned.1.call-start = ((), (), s32[]{:S(2)}) async-start(), calls=%async_computation.16 | async-start | bytes 2293760 | tf_op jit(solution)/shard_map/reduce_scatter | solution.py:134
  80.7 116.9 %reduce-scatter.17.cloned.1.call-start = ((), (), s32[]{:S(2)}) async-start(), calls=%async_computation.11 | async-start | bytes 2293760 | tf_op jit(solution)/shard_map/reduce_scatter | solution.py:61
  88.9 8.4 %copy-start.16 = (s32[8]{0:T(128)S(1)}, s32[8]{0:T(128)}, u32[]{:S(2)}) copy-start(s32[8]{0:T(128)} %param.24) | copy-start | bytes 100
  89.0 10.9 %copy-start.7 = (bf16[64,2048]{1,0:T(8,128)(2,1)S(1)}, bf16[64,2048]{1,0:T(8,128)(2,1)}, u32[]{:S(2)}) copy-start(bf16[64,2048]{1,0:T(8,128)(2,1)} %param.14) | copy-start | bytes 786436
  89.0 144.7 %reduce-scatter.19.cloned.1.call-start = ((), (), s32[]{:S(2)}) async-start(), calls=%async_computation.12 | async-start | bytes 2293760 | tf_op jit(solution)/shard_map/reduce_scatter | solution.py:64
  97.2 29.0 %copy-start.4 = (bf16[16,1792,16]{1,2,0:T(8,128)(2,1)S(1)}, bf16[16,1792,16]{1,2,0:T(8,128)(2,1)}, u32[]{:S(2)}) copy-start(bf16[16,1792,16]{1,2,0:T(8,128)(2,1)} %param.23) | copy-start | bytes 2752516
  97.2 173.1 %all-gather.7.cloned.1.call-start = ((), (), s32[]{:S(2)}) async-start(), calls=%async_computation.13 | async-start | bytes 2293760 | tf_op jit(solution)/shard_map/all_gather | solution.py:85
  125.2 0.7 copy-start.10
  128.5 69.0 %copy-start.12 = (bf16[2,16,1792]{2,1,0:T(8,128)(2,1)}, bf16[2,16,1792]{2,1,0:T(8,128)(2,1)S(1)}, u32[]{:S(2)}) copy-start(bf16[2,16,1792]{2,1,0:T(8,128)(2,1)S(1)} %gather_fusion.1) | copy-start | bytes 344068
  237.0 38.8 %copy-start.6 = (bf16[128,1792]{1,0:T(8,128)(2,1)}, bf16[128,1792]{1,0:T(8,128)(2,1)S(1)}, u32[]{:S(2)}) copy-start(bf16[128,1792]{1,0:T(8,128)(2,1)S(1)} %get-tuple-element.45) | copy-start | bytes 1376260
  237.1 0.7 copy-start.1
  237.1 1.3 copy-start.14
  237.1 66.4 %reduce-scatter.35.cloned.1.call-start = ((), (), s32[]{:S(2)}) async-start(), calls=%async_computation.22 | async-start | bytes 147456
  272.4 3.4 copy-start.13
  273.2 99.3 %reduce-scatter.27.cloned.1.call-start = ((), (), s32[]{:S(2)}) async-start(), calls=%async_computation.18 | async-start | bytes 1146880 | tf_op jit(solution)/shard_map/reduce_scatter | solution.py:175
  275.8 98.6 %reduce-scatter.29.cloned.1.call-start = ((), (), s32[]{:S(2)}) async-start(), calls=%async_computation.19 | async-start | bytes 1146880 | tf_op jit(solution)/shard_map/reduce_scatter | solution.py:178
  276.1 27.5 %copy-start.8 = (bf16[64,2048]{1,0:T(8,128)(2,1)S(1)}, bf16[64,2048]{1,0:T(8,128)(2,1)}, u32[]{:S(2)}) copy-start(bf16[64,2048]{1,0:T(8,128)(2,1)} %param.14) | copy-start | bytes 786436
  278.4 27.3 %copy-start.9 = (bf16[512,1792]{1,0:T(8,128)(2,1)S(1)}, bf16[512,1792]{1,0:T(8,128)(2,1)}, u32[]{:S(2)}) copy-start(bf16[512,1792]{1,0:T(8,128)(2,1)} %all-gather.7.cloned.1.call-done) | copy-start | bytes 5505028
  278.5 118.1 %reduce-scatter.25.cloned.1.call-start = ((), (), s32[]{:S(2)}) async-start(), calls=%async_computation.17 | async-start | bytes 1179648 | tf_op jit(solution)/shard_map/reduce_scatter | solution.py:124
  305.7 127.3 %reduce-scatter.21.cloned.1.call-start = ((), (), s32[]{:S(2)}) async-start(), calls=%async_computation.14 | async-start | bytes 2359296 | tf_op jit(solution)/shard_map/reduce_scatter | solution.py:94
  305.7 8.3 %copy-start.11 = (bf16[1,512,16]{2,0,1:T(2,128)(2,1)S(1)}, bf16[1,512,16]{2,0,1:T(2,128)(2,1)}, u32[]{:S(2)}) copy-start(bf16[1,512,16]{2,0,1:T(2,128)(2,1)} %copy-done.10) | copy-start | bytes 49156
  314.0 56.2 %copy-start.3 = (bf16[512,2048]{1,0:T(8,128)(2,1)S(1)}, bf16[512,2048]{1,0:T(8,128)(2,1)}, u32[]{:S(2)}) copy-start(bf16[512,2048]{1,0:T(8,128)(2,1)} %all-gather.5.cloned.1.call-done) | copy-start | bytes 6291460
  376.1 56.9 %copy-start.15 = (bf16[64,16]{1,0:T(8,128)(2,1)S(1)}, bf16[64,16]{1,0:T(8,128)(2,1)}, u32[]{:S(2)}) copy-start(bf16[64,16]{1,0:T(8,128)(2,1)} %reduce-scatter.35.cloned.1.call-done) | copy-start | bytes 6148
Sparse Core Ops, SparseCore 0:
  9.6 31.7 all-gather.4
  43.0 28.5 all-gather.8
  75.0 23.3 reduce-scatter.30
  101.8 23.8 reduce-scatter.32
  128.6 33.0 reduce-scatter.22
  164.5 32.9 reduce-scatter.16
  200.6 32.9 reduce-scatter.18
  237.2 33.1 all-gather.6
  273.4 30.1 reduce-scatter.34
  306.6 25.0 reduce-scatter.26
  334.9 26.9 reduce-scatter.28
  364.1 32.4 reduce-scatter.24
  399.0 33.9 reduce-scatter.20
where the time goes:
time: 443 us; the launch traced here: 441 us
  waiting for transfers between devices  262 us (59%)
  blocking collectives  66.3 us (15%)
  matrix products  59.7 us (13%)
  other arithmetic  21.4 us (5%)
  between operations  16.1 us (4%)
  local copies, waits for them, and re-layouts  14.9 us (3%)
    reduce_scatter x1, waiting for transfers between devices, shards(): lax.psum_scatter(up_part.astype(jnp.bfloat16), 'dp', scatter_dimension=0,...  36.1 us
    reduce_scatter x1, waiting for transfers between devices, shards(): lax.psum_scatter(gate_part.astype(jnp.bfloat16), 'dp', scatter_dimension=...  35.9 us
    reduce_scatter x1, waiting for transfers between devices, shards(): lax.psum_scatter(out_part.astype(jnp.bfloat16), 'tensor', scatter_dimensi...  34.8 us
    all_gather x1, waiting for transfers between devices, shards(): all_hidden = lax.all_gather(hidden, 'dp', axis=0, tiled=True)  30.7 us
    all_gather x1, waiting for transfers between devices, shards(): all_inputs = lax.all_gather(tokens, 'tensor', axis=0, tiled=True)  30.3 us
    reduce_scatter x1, waiting for transfers between devices, shards(): lax.psum_scatter(hidden_grad_part.astype(jnp.bfloat16), 'dp', scatter_dim...  26.9 us
    psum x1, blocking collectives, shards(): lax.psum((gate_backward_piece, up_backward_piece), 'tensor')  26 us
    unnamed x16, waiting for transfers between devices  25.8 us
  transfers between devices with their start and end apart: 13, of which 9 were waited for; matrix products, arithmetic and copies ran while one was open for 20% of the time, Pallas kernels for 0%

commit v1 on v0

v1 whole, which is shorter than its diff:
```python
import jax
import jax.numpy as jnp
from jax import lax
from jax.sharding import PartitionSpec as P

BLOCK = 64


adapter_scale = 0.5


def dot(a, b, ca=1, cb=0, precision=None):
    return lax.dot_general(
        a,
        b,
        (((ca,), (cb,)), ((), ())),
        preferred_element_type=jnp.float32,
        precision=precision,
    )


def flip(x, axis, bits):
    n = lax.axis_size(axis)
    return lax.ppermute(x, axis, [(i, i ^ bits) for i in range(n)])


def rows(x, index, count):
    return lax.dynamic_slice_in_dim(x, index * count, count)


def put(whole, x, index):
    return lax.dynamic_update_slice_in_dim(whole, x, index * x.shape[0], 0)


def gather_far(x, axis, step):
    return {b: x if b == 0 else flip(x, axis, b) for b in range(0, lax.axis_size(axis), step)}


def gather_tensor(x):
    me = lax.axis_index("tensor")
    held = gather_far(x, "tensor", 2)
    whole = jnp.zeros((x.shape[0] * lax.axis_size("tensor"),) + x.shape[1:], x.dtype)
    for b, block in held.items():
        whole = put(whole, block, me ^ b)
        whole = put(whole, flip(block, "tensor", 1), me ^ b ^ 1)
    return whole


def gather_dp(x):
    me = lax.axis_index("dp")
    whole = jnp.zeros((x.shape[0] * lax.axis_size("dp"),) + x.shape[1:], x.dtype)
    for b, block in gather_far(x, "dp", 1).items():
        whole = put(whole, block, me ^ b)
    return whole


def scatter_dp(x):
    n = lax.axis_size("dp")
    me = lax.axis_index("dp")
    count = x.shape[0] // n
    got = [flip(rows(x, me ^ b, count), "dp", b) for b in range(n - 1, 0, -1)]
    total = rows(x, me, count).astype(jnp.float32)
    for piece in got:
        total = total + piece.astype(jnp.float32)
    return total


def scatter_tensor(x):
    n = lax.axis_size("tensor")
    me = lax.axis_index("tensor")
    count = x.shape[0] // n
    total = None
    for b in range(n - 2, -1, -2):
        mate = flip(rows(x, me ^ b ^ 1, count), "tensor", 1).astype(jnp.float32)
        pair = rows(x, me ^ b, count).astype(jnp.float32) + mate
        if b:
            pair = flip(pair.astype(x.dtype), "tensor", b).astype(jnp.float32)
        total = pair if total is None else total + pair
    return total


def sum_all(x, axis):
    bits = 1
    while bits < lax.axis_size(axis):
        x = x + flip(x, axis, bits)
        bits *= 2
    return x


def shards(
    tokens,
    cotangent,
    gate_weight,
    up_weight,
    down_weight,
    gate_in,
    up_in,
    down_out,
    gate_out,
    up_out,
    down_in,
    tenants,
    owners,
):
    highest = lax.Precision.HIGHEST
    dp_count = lax.axis_size("dp")
    tensor_count = lax.axis_size("tensor")
    dp_index = lax.axis_index("dp")
    tensor_index = lax.axis_index("tensor")
    rows_in, feat_here = tokens.shape
    width_here = gate_weight.shape[1]
    rank = gate_in.shape[2]
    token_count = rows_in * tensor_count
    group_rows = token_count // dp_count
    blocks_all = tenants.shape[0]
    blocks_group = group_rows // BLOCK
    blocks_in = rows_in // BLOCK
    tenant_count = owners.shape[0]
    slots_here = tenant_count // dp_count
    tenants_here = tenant_count // tensor_count
    columns = tenant_count * rank
    bf16 = jnp.bfloat16

    def pick(table, index):
        at = jnp.arange(table.shape[0], dtype=jnp.int32)
        return jnp.sum(jnp.where(index[:, None] == at[None, :], table[None, :], 0), axis=1)

    def mask_of(block_values, first, count):
        n = block_values.shape[0]
        column = lax.broadcasted_iota(jnp.int32, (n, BLOCK, count * rank), 2) // rank + first
        return (block_values[:, None, None] == column).reshape(n * BLOCK, count * rank)

    def tile(count):
        r = lax.broadcasted_iota(jnp.int32, (rank, count * rank), 0)
        c = lax.broadcasted_iota(jnp.int32, (rank, count * rank), 1)
        return (c % rank == r).astype(bf16)

    def expand(r, mask):
        wide = dot(r, tile(mask.shape[1] // rank))
        return jnp.where(mask, wide, 0.0).astype(bf16)

    def collapse(wide, mask):
        narrow = jnp.where(mask, wide, jnp.zeros_like(wide))
        t = tile(mask.shape[1] // rank).astype(wide.dtype)
        return dot(narrow, t, 1, 1, highest if wide.dtype == jnp.float32 else None)

    def as_rows(table):
        return table.transpose(0, 2, 1).reshape(columns, table.shape[1])

    arange = lambda n: jnp.arange(n, dtype=jnp.int32)
    group_tenants = pick(tenants, dp_index * blocks_group + arange(blocks_group))
    input_tenants = pick(tenants, tensor_index * blocks_in + arange(blocks_in))
    block_slots = pick(owners, tenants)
    mask_all = mask_of(tenants, 0, tenant_count)
    mask_group = mask_of(group_tenants, 0, tenant_count)
    mask_input = mask_of(input_tenants, 0, tenant_count)
    mask_held = mask_of(tenants, tensor_index * tenants_here, tenants_here)
    mask_slots = mask_of(block_slots, dp_index * slots_here, slots_here)
    mask_local = mask_of(arange(blocks_group), 0, blocks_group)
    gate_raise = gate_out.reshape(columns, width_here)
    up_raise = up_out.reshape(columns, width_here)
    down_raise = down_out.reshape(columns, feat_here)

    all_inputs = gather_tensor(tokens)
    all_cot = gather_tensor(cotangent)

    gate_sum = scatter_dp(dot(all_inputs, gate_weight).astype(bf16))
    rank_parts = jnp.concatenate(
        [
            collapse(dot(all_inputs, as_rows(table), 1, 1).astype(bf16), mask_all)
            for table in (gate_in, up_in)
        ],
        axis=1,
    ).astype(bf16)
    ranks = scatter_dp(rank_parts).astype(bf16)
    gate_rank, up_rank = ranks[:, :rank], ranks[:, rank:]
    up_sum = scatter_dp(dot(all_inputs, up_weight).astype(bf16))

    gate_full = gate_sum + adapter_scale * dot(expand(gate_rank, mask_group), gate_raise)
    up_full = up_sum + adapter_scale * dot(expand(up_rank, mask_group), up_raise)
    hidden = (jax.nn.silu(gate_full) * up_full).astype(bf16)
    all_hidden = gather_dp(hidden)

    down_back = adapter_scale * collapse(dot(all_cot, down_raise, 1, 1), mask_all)
    down_back = sum_all(down_back, "dp").astype(bf16)
    group_down_back = rows(down_back, dp_index, group_rows)
    down_drop = as_rows(down_in)
    hidden_grad = scatter_dp(dot(all_cot, down_weight, 1, 1).astype(bf16))
    hidden_grad = hidden_grad + dot(expand(group_down_back, mask_group), down_drop)

    out_sum = scatter_tensor(dot(all_hidden, down_weight).astype(bf16))
    down_rank = collapse(dot(all_hidden, down_drop, 1, 1).astype(bf16), mask_all)
    down_rank = sum_all(down_rank, "tensor").astype(bf16)
    own_down_rank = rows(down_rank, tensor_index, rows_in)
    mixed = (
        out_sum + adapter_scale * dot(expand(own_down_rank, mask_input), down_raise)
    ).astype(bf16)
    grad_down_out = adapter_scale * dot(expand(down_rank, mask_held), all_cot, 0, 0)
    grad_down_out = grad_down_out.reshape(tenants_here, rank, feat_here)

    sig = jax.nn.sigmoid(gate_full)
    up_grad = (hidden_grad * gate_full * sig).astype(bf16)
    gate_grad = (hidden_grad * up_full * sig * (1.0 + gate_full * (1.0 - sig))).astype(bf16)
    backs = adapter_scale * jnp.concatenate(
        [
            collapse(dot(gate_grad, gate_raise, 1, 1), mask_group),
            collapse(dot(up_grad, up_raise, 1, 1), mask_group),
        ],
        axis=1,
    )
    backs = gather_dp(sum_all(backs, "tensor").astype(bf16))

    lifts = adapter_scale * jnp.concatenate(
        [
            dot(expand(gate_rank, mask_local), gate_grad, 0, 0),
            dot(expand(up_rank, mask_local), up_grad, 0, 0),
        ],
        axis=0,
    )
    lifts = gather_dp(lifts.astype(bf16))

    def own_lift(which):
        shape = (slots_here, rank, dp_count, 2, blocks_group, rank)
        iota = lambda axis: lax.broadcasted_iota(jnp.int32, shape, axis)
        slots = block_slots.reshape(1, 1, dp_count, 1, blocks_group, 1)
        chosen = (
            (iota(0) + dp_index * slots_here == slots) & (iota(1) == iota(5)) & (iota(3) == which)
        )
        chosen = chosen.astype(bf16).reshape(slots_here * rank, lifts.shape[0])
        return dot(chosen, lifts).reshape(slots_here, rank, width_here)

    grad_gate_out = own_lift(0)
    grad_up_out = own_lift(1)

    def own_in(back, mask, source, count):
        grad = dot(expand(back, mask), source, 0, 0)
        return grad.reshape(count, rank, source.shape[1]).transpose(0, 2, 1)

    grad_gate_in = own_in(backs[:, :rank], mask_held, all_inputs, tenants_here)
    grad_up_in = own_in(backs[:, rank:], mask_held, all_inputs, tenants_here)
    grad_down_in = own_in(down_back, mask_slots, all_hidden, slots_here)
    return (
        mixed,
        grad_gate_in,
        grad_up_in,
        grad_down_out,
        grad_gate_out,
        grad_up_out,
        grad_down_in,
    )


def solution(mesh):
    in_specs = (
        P("tensor", "dp"),
        P("tensor", "dp"),
        P("dp", "tensor"),
        P("dp", "tensor"),
        P("tensor", "dp"),
        P(None, "dp", None),
        P(None, "dp", None),
        P(None, None, "dp"),
        P(None, None, "tensor"),
        P(None, None, "tensor"),
        P(None, "tensor", None),
        P(),
        P(),
    )
    out_specs = (
        P("tensor", "dp"),
        P("tensor", "dp", None),
        P("tensor", "dp", None),
        P("tensor", None, "dp"),
        P("dp", None, "tensor"),
        P("dp", None, "tensor"),
        P("dp", "tensor", None),
    )
    return jax.shard_map(shards, mesh=mesh, in_specs=in_specs, out_specs=out_specs, check_vma=False)
```

time: 443 us -> 262 us (0.59)
  waiting for transfers between devices: 262 us -> 88.3 us
  blocking collectives: 66.3 us -> 0 us
  starting transfers between devices: 0.71 us -> 60.4 us
  local copies, waits for them, and re-layouts: 14.9 us -> 36.1 us
  between operations: 16.1 us -> 1.25 us
  other arithmetic: 21.4 us -> 13.3 us
    reduce_scatter x7 -> x0, waiting for transfers between devices: 151 us -> none  [the longest x1 36.1 us: shards(): lax.psum_scatter(up_part.astype(jnp.bfloat16), 'dp', scatter_dimension=0,...]
    ppermute x0 -> x50, waiting for transfers between devices: none -> 88.3 us  [flip(): return lax.ppermute(x, axis, [(i, i ^ bits) for i in range(n)])]
    all_gather x3 -> x0, waiting for transfers between devices: 85 us -> none  [the longest x1 30.7 us: shards(): all_hidden = lax.all_gather(hidden, 'dp', axis=0, tiled=True)]
    ppermute x0 -> x50, starting transfers between devices: none -> 60.4 us  [flip(): return lax.ppermute(x, axis, [(i, i ^ bits) for i in range(n)])]
    psum x2 -> x0, blocking collectives: 36.1 us -> none  [the longest x1 26 us: shards(): lax.psum((gate_backward_piece, up_backward_piece), 'tensor')]
    all_gather x3 -> x0, blocking collectives: 30.3 us -> none  [the longest x1 14.2 us: shards(): lax.all_gather(down_backward.reshape(rows_in, rank_width), 'tensor', axis...]
    unnamed x16 -> x0, waiting for transfers between devices: 25.8 us -> none
    dynamic_update_slice x0 -> x25, local copies, waits for them, and re-layouts: none -> 21.7 us  [put(): return lax.dynamic_update_slice_in_dim(whole, x, index * x.shape[0], 0)]
  transfers between devices with their start and end apart: 13 -> 50, of which waited for: 9 -> 15; matrix products, arithmetic and copies ran while one was open for 20% -> 36% of each run, Pallas kernels for 0% -> 0%
where the time goes in v1:
time: 262 us; the launch traced here: 260 us
  waiting for transfers between devices  88.3 us (34%)
  matrix products  60.9 us (23%)
  starting transfers between devices  60.4 us (23%)
  local copies, waits for them, and re-layouts  36.1 us (14%)
  other arithmetic  13.3 us (5%)
    ppermute x50, waiting for transfers between devices, flip(): return lax.ppermute(x, axis, [(i, i ^ bits) for i in range(n)])  88.3 us
    dot_general x25, matrix products, dot(): lax.dot_general(a, b, (((ca,), (cb,)), ((), ())), preferred_element_type=...  60.9 us
    ppermute x50, starting transfers between devices, flip(): return lax.ppermute(x, axis, [(i, i ^ bits) for i in range(n)])  60.4 us
    dynamic_update_slice x25, local copies, waits for them, and re-layouts, put(): return lax.dynamic_update_slice_in_dim(whole, x, index * x.shape[0], 0)  21.7 us
  transfers between devices with their start and end apart: 50, of which 15 were waited for; matrix products, arithmetic and copies ran while one was open for 36% of the time, Pallas kernels for 0%

profile of v1, /device:TPU:0, one launch (start us, length us, event | category | flops | bytes accessed | tf_op | source)
XLA Modules:
  0.0 260.2 jit_solution(16037475663141090637)
XLA Ops:
  1.2 2.7 %collective-permute-start.1 = (bf16[64,2048]{1,0:T(8,128)(2,1)}, bf16[64,2048]{1,0:T(8,128)(2,1)}, u32[]{:S(2)}, u32[]{:S(2)}) collective-permute-start(bf16[64,2048]{1,0:T(8,128)(2,1)} %param.13), channel_id=1, source_target_pairs={{0,2},{1,3},{2,0},{3,1},{4,6},{5,7},{6,4},{7,5},{8,10},{9,11},{10,... | collective-permute-start | bytes 786440 | tf_op jit(solution)/shard_map/ppermute | solution.py:24
  3.8 2.6 collective-permute-start.3
  17.5 3.6 %collective-permute-start.32 = (bf16[64,2048]{1,0:T(8,128)(2,1)S(1)}, bf16[64,2048]{1,0:T(8,128)(2,1)}, u32[]{:S(2)}, u32[]{:S(2)}) collective-permute-start(bf16[64,2048]{1,0:T(8,128)(2,1)S(1)} %copy-done.13), channel_id=1, source_target_pairs={{0,4},{1,5},{2,6},{3,7},{4,0},{5,1},{6,2},{7,3},{8,12},{9,13},{10,... | collective-permute-start | bytes 786440 | tf_op jit(solution)/shard_map/ppermute | solution.py:24
  22.1 8.5 %collective-permute-done.30 = bf16[64,2048]{1,0:T(8,128)(2,1)} collective-permute-done((bf16[64,2048]{1,0:T(8,128)(2,1)S(1)}, bf16[64,2048]{1,0:T(8,128)(2,1)}, u32[]{:S(2)}, u32[]{:S(2)}) %collective-permute-start.30) | collective-permute-done | bytes 262176 | tf_op jit(solution)/shard_map/ppermute | solution.py:24
  34.5 13.5 %collective-permute-done.32 = bf16[64,2048]{1,0:T(8,128)(2,1)} collective-permute-done((bf16[64,2048]{1,0:T(8,128)(2,1)S(1)}, bf16[64,2048]{1,0:T(8,128)(2,1)}, u32[]{:S(2)}, u32[]{:S(2)}) %collective-permute-start.32) | collective-permute-done | bytes 262176 | tf_op jit(solution)/shard_map/ppermute | solution.py:24
  55.1 2.5 collective-permute-start.10
  70.5 7.0 %convolution_convert_fusion.2 = bf16[512,1792]{1,0:T(8,128)(2,1)S(1)} fusion(bf16[512,2048]{1,0:T(8,128)(2,1)S(1)} %constant_dynamic-update-slice_fusion.20, bf16[2048,1792]{1,0:T(8,128)(2,1)} %param.16), kind=kOutput, calls=%fused_computation.2 | convolution fusion | flops 3759013888 | bytes 11272192 | tf_op jit(solution)/shard_map/dot_general | solution.py:13
  80.4 3.9 %convolution_convert_fusion.3 = bf16[512,1792]{1,0:T(8,128)(2,1)S(1)} fusion(bf16[512,2048]{1,0:T(8,128)(2,1)S(1)} %constant_dynamic-update-slice_fusion.20, bf16[2048,1792]{1,0:T(8,128)(2,1)S(1)} %bitcast.75), kind=kOutput, calls=%fused_computation.3 | convolution fusion | flops 3759013888 | bytes 11272192 | tf_op jit(solution)/shard_map/dot_general | solution.py:13
  86.8 5.8 %convolution_convert_fusion = bf16[512,1792]{1,0:T(8,128)(2,1)S(1)} fusion(bf16[512,2048]{1,0:T(8,128)(2,1)} %constant_dynamic-update-slice_fusion.8, bf16[1792,2048]{1,0:T(8,128)(2,1)S(1)} %bitcast.77), kind=kOutput, calls=%fused_computation | convolution fusion | flops 3759013888 | bytes 11272192 | tf_op jit(solution)/shard_map/dot_general | solution.py:13
  98.5 2.6 convolution_multiply_fusion
  101.7 2.5 convolution_multiply_fusion.1
  104.2 5.9 %collective-permute-done.40 = f32[512,16]{0,1:T(8,128)S(1)} collective-permute-done((f32[512,16]{0,1:T(8,128)S(1)}, f32[512,16]{0,1:T(8,128)S(1)}, u32[]{:S(2)}, u32[]{:S(2)}) %collective-permute-start.40) | collective-permute-done | bytes 32800 | tf_op jit(solution)/shard_map/ppermute | solution.py:24
  114.1 6.1 %collective-permute-done.7 = bf16[128,1792]{1,0:T(8,128)(2,1)} collective-permute-done((bf16[128,1792]{1,0:T(8,128)(2,1)}, bf16[128,1792]{1,0:T(8,128)(2,1)}, u32[]{:S(2)}, u32[]{:S(2)}) %collective-permute-start.7) | collective-permute-done | bytes 458784 | tf_op jit(solution)/shard_map/ppermute | solution.py:24
  121.3 2.6 fusion.11
  123.9 11.2 %collective-permute-done.8 = bf16[128,1792]{1,0:T(8,128)(2,1)} collective-permute-done((bf16[128,1792]{1,0:T(8,128)(2,1)}, bf16[128,1792]{1,0:T(8,128)(2,1)}, u32[]{:S(2)}, u32[]{:S(2)}) %collective-permute-start.8) | collective-permute-done | bytes 458784 | tf_op jit(solution)/shard_map/ppermute | solution.py:24
  135.2 4.7 %collective-permute-done.36 = bf16[128,1792]{1,0:T(8,128)(2,1)} collective-permute-done((bf16[128,1792]{1,0:T(8,128)(2,1)}, bf16[128,1792]{1,0:T(8,128)(2,1)}, u32[]{:S(2)}, u32[]{:S(2)}) %collective-permute-start.36) | collective-permute-done | bytes 458784 | tf_op jit(solution)/shard_map/ppermute | solution.py:24
  139.8 6.9 %collective-permute-done.37 = bf16[128,1792]{1,0:T(8,128)(2,1)} collective-permute-done((bf16[128,1792]{1,0:T(8,128)(2,1)}, bf16[128,1792]{1,0:T(8,128)(2,1)}, u32[]{:S(2)}, u32[]{:S(2)}) %collective-permute-start.37) | collective-permute-done | bytes 458784 | tf_op jit(solution)/shard_map/ppermute | solution.py:24
  146.7 4.4 %multiply_convert_fusion.1 = (bf16[128,1792]{1,0:T(8,128)(2,1)S(1)}, f32[128,1792]{1,0:T(8,128)S(1)}, f32[128,1792]{1,0:T(8,128)S(1)}, f32[128,1792]{1,0:T(8,128)S(1)}) fusion(f32[128,1792]{1,0:T(8,128)} %fusion.11, bf16[128,1792]{1,0:T(8,128)(2,1)} %collective-permute-done.38, bf16[128,1792]{1,0:T(8,128)(2,1)} %collective-permute-done.37, ...), kind=kLoop, calls=%fused_computation.54 | loop fusion | flops 7798784 | bytes 11468804 | tf_op jit(solution)/shard_map/convert_element_type | solution.py:203
  159.7 4.9 %collective-permute-start.42 = (f32[128,32]{0,1:T(8,128)S(1)}, f32[128,32]{0,1:T(8,128)S(1)}, u32[]{:S(2)}, u32[]{:S(2)}) collective-permute-start(f32[128,32]{0,1:T(8,128)S(1)} %fusion.224), channel_id=1, source_target_pairs={{0,2},{1,3},{2,0},{3,1},{4,6},{5,7},{6,4},{7,5},{8,10},{9,11},{10,... | collective-permute-start | bytes 49160 | tf_op jit(solution)/shard_map/ppermute | solution.py:24
  166.4 3.0 %collective-permute-start.43 = (f32[128,32]{0,1:T(8,128)S(1)}, f32[128,32]{0,1:T(8,128)S(1)}, u32[]{:S(2)}, u32[]{:S(2)}) collective-permute-start(f32[128,32]{0,1:T(8,128)S(1)} %add.353), channel_id=1, source_target_pairs={{0,4},{1,5},{2,6},{3,7},{4,0},{5,1},{6,2},{7,3},{8,12},{9,13},{10,... | collective-permute-start | bytes 49160 | tf_op jit(solution)/shard_map/ppermute | solution.py:24
  176.3 3.5 %collective-permute-done.44 = bf16[128,32]{0,1:T(8,128)(2,1)S(1)} collective-permute-done((bf16[128,32]{0,1:T(8,128)(2,1)S(1)}, bf16[128,32]{0,1:T(8,128)(2,1)S(1)}, u32[]{:S(2)}, u32[]{:S(2)}) %collective-permute-start.44) | collective-permute-done | bytes 8224 | tf_op jit(solution)/shard_map/ppermute | solution.py:24
  181.0 2.5 collective-permute-done.45
  185.3 2.7 %collective-permute-done.46 = bf16[128,32]{0,1:T(8,128)(2,1)S(1)} collective-permute-done((bf16[128,32]{0,1:T(8,128)(2,1)S(1)}, bf16[128,32]{0,1:T(8,128)(2,1)S(1)}, u32[]{:S(2)}, u32[]{:S(2)}) %collective-permute-start.46) | collective-permute-done | bytes 8224 | tf_op jit(solution)/shard_map/ppermute | solution.py:24
  194.2 5.1 %collective-permute-done.48 = bf16[64,1792]{1,0:T(8,128)(2,1)} collective-permute-done((bf16[64,1792]{1,0:T(8,128)(2,1)}, bf16[64,1792]{1,0:T(8,128)(2,1)}, u32[]{:S(2)}, u32[]{:S(2)}) %collective-permute-start.48) | collective-permute-done | bytes 229408 | tf_op jit(solution)/shard_map/ppermute | solution.py:24
  211.4 7.4 %convolution_convert_fusion.1 = bf16[512,2048]{1,0:T(8,128)(2,1)S(1)} fusion(bf16[512,1792]{1,0:T(8,128)(2,1)S(1)} %constant_dynamic-update-slice_fusion.16, bf16[1792,2048]{1,0:T(8,128)(2,1)} %param.17), kind=kOutput, calls=%fused_computation.1 | convolution fusion | flops 3759144960 | bytes 11272192 | tf_op jit(solution)/shard_map/dot_general | solution.py:13
  218.9 5.0 %collective-permute-start.27 = (f32[512,16]{0,1:T(8,128)S(1)}, f32[512,16]{0,1:T(8,128)S(1)}, u32[]{:S(2)}, u32[]{:S(2)}) collective-permute-start(f32[512,16]{0,1:T(8,128)S(1)} %add.339), channel_id=1, source_target_pairs={{0,2},{1,3},{2,0},{3,1},{4,6},{5,7},{6,4},{7,5},{8,10},{9,11},{10,... | collective-permute-start | bytes 98312 | tf_op jit(solution)/shard_map/ppermute | solution.py:24
  225.8 3.0 %collective-permute-start.28 = (f32[512,16]{0,1:T(8,128)S(1)}, f32[512,16]{0,1:T(8,128)S(1)}, u32[]{:S(2)}, u32[]{:S(2)}) collective-permute-start(f32[512,16]{0,1:T(8,128)S(1)} %add.340), channel_id=1, source_target_pairs={{0,4},{1,5},{2,6},{3,7},{4,0},{5,1},{6,2},{7,3},{8,12},{9,13},{10,... | collective-permute-start | bytes 98312 | tf_op jit(solution)/shard_map/ppermute | solution.py:24
  232.7 2.5 collective-permute-start.20
  237.2 2.9 %convolution_multiply_fusion.3 = f32[32,2048]{1,0:T(8,128)} fusion(bf16[512,2048]{1,0:T(8,128)(2,1)} %constant_dynamic-update-slice_fusion.8, bf16[512,16]{0,1:T(8,128)(2,1)S(1)} %add_convert_fusion.5, s32[]{:T(128)S(6)} %mul.177, s32[32]{0:T(128)S(1)} %get-tuple-element.46, s32[32]{0:T(128)S(1)} %get-tuple-element.49, s32[512]{0:T(512)S(1)} %eq.234, ...), kind=kOutput, calls=%fused_computation.7 | convolution fusion | flops 67781632 | bytes 2378308 | tf_op jit(solution)/shard_map/dot_general | solution.py:13
  240.1 3.8 %collective-permute-done.20 = bf16[64,2048]{1,0:T(8,128)(2,1)S(1)} collective-permute-done((bf16[64,2048]{1,0:T(8,128)(2,1)S(1)}, bf16[64,2048]{1,0:T(8,128)(2,1)S(1)}, u32[]{:S(2)}, u32[]{:S(2)}) %collective-permute-start.20) | collective-permute-done | bytes 262176 | tf_op jit(solution)/shard_map/ppermute | solution.py:24
  243.9 13.4 %collective-permute-done.22 = bf16[64,2048]{1,0:T(8,128)(2,1)S(1)} collective-permute-done((bf16[64,2048]{1,0:T(8,128)(2,1)S(1)}, bf16[64,2048]{1,0:T(8,128)(2,1)S(1)}, u32[]{:S(2)}, u32[]{:S(2)}) %collective-permute-start.22) | collective-permute-done | bytes 262176 | tf_op jit(solution)/shard_map/ppermute | solution.py:24
  257.3 2.9 %add_convert_fusion = bf16[64,2048]{1,0:T(8,128)(2,1)} fusion(bf16[64,2048]{1,0:T(8,128)(2,1)S(1)} %collective-permute-done.25, bf16[64,2048]{1,0:T(8,128)(2,1)S(1)} %collective-permute-done.24, bf16[64,2048]{1,0:T(8,128)(2,1)S(1)} %collective-permute-done.22, bf16[64,2048]{1,0:T(8,128)(2,1)S(1)} %collective-permute-done.20, ...), kind=kOutput, calls=%fused_computation.60 | convolution fusion | flops 69279744 | bytes 2631684 | tf_op jit(solution)/shard_map/dot_general | solution.py:13
  (226 shorter events, 99.6 us)
Async XLA Ops:
  0.7 15.0 %collective-permute-start = (bf16[64,2048]{1,0:T(8,128)(2,1)}, bf16[64,2048]{1,0:T(8,128)(2,1)}, u32[]{:S(2)}, u32[]{:S(2)}) collective-permute-start(bf16[64,2048]{1,0:T(8,128)(2,1)} %param.13), channel_id=1, source_target_pairs={{0,1},{1,0},{2,3},{3,2},{4,5},{5,4},{6,7},{7,6},{8,9},{9,8},{10,11... | collective-permute-start | bytes 786440 | tf_op jit(solution)/shard_map/ppermute | solution.py:24
  1.2 16.3 %collective-permute-start.1 = (bf16[64,2048]{1,0:T(8,128)(2,1)}, bf16[64,2048]{1,0:T(8,128)(2,1)}, u32[]{:S(2)}, u32[]{:S(2)}) collective-permute-start(bf16[64,2048]{1,0:T(8,128)(2,1)} %param.13), channel_id=1, source_target_pairs={{0,2},{1,3},{2,0},{3,1},{4,6},{5,7},{6,4},{7,5},{8,10},{9,11},{10,... | collective-permute-start | bytes 786440 | tf_op jit(solution)/shard_map/ppermute | solution.py:24
  3.8 30.1 %collective-permute-start.3 = (bf16[64,2048]{1,0:T(8,128)(2,1)}, bf16[64,2048]{1,0:T(8,128)(2,1)}, u32[]{:S(2)}, u32[]{:S(2)}) collective-permute-start(bf16[64,2048]{1,0:T(8,128)(2,1)} %param.13), channel_id=1, source_target_pairs={{0,4},{1,5},{2,6},{3,7},{4,0},{5,1},{6,2},{7,3},{8,12},{9,13},{10,... | collective-permute-start | bytes 786440 | tf_op jit(solution)/shard_map/ppermute | solution.py:24
  6.4 28.0 %collective-permute-start.5 = (bf16[64,2048]{1,0:T(8,128)(2,1)}, bf16[64,2048]{1,0:T(8,128)(2,1)}, u32[]{:S(2)}, u32[]{:S(2)}) collective-permute-start(bf16[64,2048]{1,0:T(8,128)(2,1)} %param.13), channel_id=1, source_target_pairs={{0,6},{1,7},{2,4},{3,5},{4,2},{5,3},{6,0},{7,1},{8,14},{9,15},{10,... | collective-permute-start | bytes 786440 | tf_op jit(solution)/shard_map/ppermute | solution.py:24
  6.4 15.6 %collective-permute-start.29 = (bf16[64,2048]{1,0:T(8,128)(2,1)}, bf16[64,2048]{1,0:T(8,128)(2,1)}, u32[]{:S(2)}, u32[]{:S(2)}) collective-permute-start(bf16[64,2048]{1,0:T(8,128)(2,1)} %param.14), channel_id=1, source_target_pairs={{0,1},{1,0},{2,3},{3,2},{4,5},{5,4},{6,7},{7,6},{8,9},{9,8},{10,11... | collective-permute-start | bytes 786440 | tf_op jit(solution)/shard_map/ppermute | solution.py:24
  15.6 15.0 %collective-permute-start.30 = (bf16[64,2048]{1,0:T(8,128)(2,1)S(1)}, bf16[64,2048]{1,0:T(8,128)(2,1)}, u32[]{:S(2)}, u32[]{:S(2)}) collective-permute-start(bf16[64,2048]{1,0:T(8,128)(2,1)S(1)} %copy-done.13), channel_id=1, source_target_pairs={{0,2},{1,3},{2,0},{3,1},{4,6},{5,7},{6,4},{7,5},{8,10},{9,11},{10,... | collective-permute-start | bytes 786440 | tf_op jit(solution)/shard_map/ppermute | solution.py:24
  17.5 30.5 %collective-permute-start.32 = (bf16[64,2048]{1,0:T(8,128)(2,1)S(1)}, bf16[64,2048]{1,0:T(8,128)(2,1)}, u32[]{:S(2)}, u32[]{:S(2)}) collective-permute-start(bf16[64,2048]{1,0:T(8,128)(2,1)S(1)} %copy-done.13), channel_id=1, source_target_pairs={{0,4},{1,5},{2,6},{3,7},{4,0},{5,1},{6,2},{7,3},{8,12},{9,13},{10,... | collective-permute-start | bytes 786440 | tf_op jit(solution)/shard_map/ppermute | solution.py:24
  22.0 25.9 %collective-permute-start.34 = (bf16[64,2048]{1,0:T(8,128)(2,1)S(1)}, bf16[64,2048]{1,0:T(8,128)(2,1)}, u32[]{:S(2)}, u32[]{:S(2)}) collective-permute-start(bf16[64,2048]{1,0:T(8,128)(2,1)S(1)} %copy-done.13), channel_id=1, source_target_pairs={{0,6},{1,7},{2,4},{3,5},{4,2},{5,3},{6,0},{7,1},{8,14},{9,15},{10,... | collective-permute-start | bytes 786440 | tf_op jit(solution)/shard_map/ppermute | solution.py:24
  30.6 17.9 %collective-permute-start.2 = (bf16[64,2048]{1,0:T(8,128)(2,1)}, bf16[64,2048]{1,0:T(8,128)(2,1)S(1)}, u32[]{:S(2)}, u32[]{:S(2)}) collective-permute-start(bf16[64,2048]{1,0:T(8,128)(2,1)} %collective-permute-done.1), channel_id=1, source_target_pairs={{0,1},{1,0},{2,3},{3,2},{4,5},{5,4},{6,7},{7,6},{8,9},{9,8},{10,11... | collective-permute-start | bytes 786440 | tf_op jit(solution)/shard_map/ppermute | solution.py:24
  34.0 24.2 %collective-permute-start.31 = (bf16[64,2048]{1,0:T(8,128)(2,1)}, bf16[64,2048]{1,0:T(8,128)(2,1)}, u32[]{:S(2)}, u32[]{:S(2)}) collective-permute-start(bf16[64,2048]{1,0:T(8,128)(2,1)} %collective-permute-done.30), channel_id=1, source_target_pairs={{0,1},{1,0},{2,3},{3,2},{4,5},{5,4},{6,7},{7,6},{8,9},{9,8},{10,11... | collective-permute-start | bytes 786440 | tf_op jit(solution)/shard_map/ppermute | solution.py:24
  34.5 15.1 %collective-permute-start.4 = (bf16[64,2048]{1,0:T(8,128)(2,1)}, bf16[64,2048]{1,0:T(8,128)(2,1)S(1)}, u32[]{:S(2)}, u32[]{:S(2)}) collective-permute-start(bf16[64,2048]{1,0:T(8,128)(2,1)} %collective-permute-done.3), channel_id=1, source_target_pairs={{0,1},{1,0},{2,3},{3,2},{4,5},{5,4},{6,7},{7,6},{8,9},{9,8},{10,11... | collective-permute-start | bytes 786440 | tf_op jit(solution)/shard_map/ppermute | solution.py:24
  48.5 16.9 %collective-permute-start.35 = (bf16[64,2048]{1,0:T(8,128)(2,1)}, bf16[64,2048]{1,0:T(8,128)(2,1)S(1)}, u32[]{:S(2)}, u32[]{:S(2)}) collective-permute-start(bf16[64,2048]{1,0:T(8,128)(2,1)} %collective-permute-done.34), channel_id=1, source_target_pairs={{0,1},{1,0},{2,3},{3,2},{4,5},{5,4},{6,7},{7,6},{8,9},{9,8},{10,11... | collective-permute-start | bytes 786440 | tf_op jit(solution)/shard_map/ppermute | solution.py:24
  55.1 39.9 %collective-permute-start.10 = (bf16[128,32]{0,1:T(8,128)(2,1)S(1)}, bf16[128,32]{0,1:T(8,128)(2,1)S(1)}, u32[]{:S(2)}, u32[]{:S(2)}) collective-permute-start(bf16[128,32]{0,1:T(8,128)(2,1)S(1)} %get-tuple-element.33), channel_id=1, source_target_pairs={{0,24},{8,16},{16,8},{24,0},{1,25},{9,17},{17,9},{25,1},{2,26},{10... | collective-permute-start | bytes 24584 | tf_op jit(solution)/shard_map/ppermute | solution.py:24
  57.6 37.9 %collective-permute-start.11 = (bf16[128,32]{0,1:T(8,128)(2,1)S(1)}, bf16[128,32]{0,1:T(8,128)(2,1)S(1)}, u32[]{:S(2)}, u32[]{:S(2)}) collective-permute-start(bf16[128,32]{0,1:T(8,128)(2,1)S(1)} %get-tuple-element.34), channel_id=1, source_target_pairs={{0,16},{8,24},{16,0},{24,8},{1,17},{9,25},{17,1},{25,9},{2,18},{10... | collective-permute-start | bytes 24584 | tf_op jit(solution)/shard_map/ppermute | solution.py:24
  58.1 38.6 %collective-permute-start.12 = (bf16[128,32]{0,1:T(8,128)(2,1)S(1)}, bf16[128,32]{0,1:T(8,128)(2,1)S(1)}, u32[]{:S(2)}, u32[]{:S(2)}) collective-permute-start(bf16[128,32]{0,1:T(8,128)(2,1)S(1)} %get-tuple-element.35), channel_id=1, source_target_pairs={{0,8},{8,0},{16,24},{24,16},{1,9},{9,1},{17,25},{25,17},{2,10},{10... | collective-permute-start | bytes 24584 | tf_op jit(solution)/shard_map/ppermute | solution.py:24
  68.9 32.2 %collective-permute-start.39 = (f32[512,16]{0,1:T(8,128)S(1)}, f32[512,16]{0,1:T(8,128)S(1)}, u32[]{:S(2)}, u32[]{:S(2)}) collective-permute-start(f32[512,16]{0,1:T(8,128)S(1)} %convolution_multiply_fusion.4), channel_id=1, source_target_pairs={{0,8},{8,0},{16,24},{24,16},{1,9},{9,1},{17,25},{25,17},{2,10},{10... | collective-permute-start | bytes 98312 | tf_op jit(solution)/shard_map/ppermute | solution.py:24
  78.7 31.9 %collective-permute-start.13 = (bf16[128,1792]{1,0:T(8,128)(2,1)}, bf16[128,1792]{1,0:T(8,128)(2,1)}, u32[]{:S(2)}, u32[]{:S(2)}) collective-permute-start(bf16[128,1792]{1,0:T(8,128)(2,1)} %get-tuple-element.24), channel_id=1, source_target_pairs={{0,24},{8,16},{16,8},{24,0},{1,25},{9,17},{17,9},{25,1},{2,26},{10... | collective-permute-start | bytes 1376264 | tf_op jit(solution)/shard_map/ppermute | solution.py:24
  95.0 16.5 %collective-permute-start.14 = (bf16[128,1792]{1,0:T(8,128)(2,1)}, bf16[128,1792]{1,0:T(8,128)(2,1)}, u32[]{:S(2)}, u32[]{:S(2)}) collective-permute-start(bf16[128,1792]{1,0:T(8,128)(2,1)} %get-tuple-element.26), channel_id=1, source_target_pairs={{0,16},{8,24},{16,0},{24,8},{1,17},{9,25},{17,1},{25,9},{2,18},{10... | collective-permute-start | bytes 1376264 | tf_op jit(solution)/shard_map/ppermute | solution.py:24
  95.5 18.0 %collective-permute-start.15 = (bf16[128,1792]{1,0:T(8,128)(2,1)}, bf16[128,1792]{1,0:T(8,128)(2,1)}, u32[]{:S(2)}, u32[]{:S(2)}) collective-permute-start(bf16[128,1792]{1,0:T(8,128)(2,1)} %get-tuple-element.25), channel_id=1, source_target_pairs={{0,8},{8,0},{16,24},{24,16},{1,9},{9,1},{17,25},{25,17},{2,10},{10... | collective-permute-start | bytes 1376264 | tf_op jit(solution)/shard_map/ppermute | solution.py:24
  96.7 23.4 %collective-permute-start.7 = (bf16[128,1792]{1,0:T(8,128)(2,1)}, bf16[128,1792]{1,0:T(8,128)(2,1)}, u32[]{:S(2)}, u32[]{:S(2)}) collective-permute-start(bf16[128,1792]{1,0:T(8,128)(2,1)} %get-tuple-element.27), channel_id=1, source_target_pairs={{0,24},{8,16},{16,8},{24,0},{1,25},{9,17},{17,9},{25,1},{2,26},{10... | collective-permute-start | bytes 1376264 | tf_op jit(solution)/shard_map/ppermute | solution.py:24
  110.1 25.1 %collective-permute-start.8 = (bf16[128,1792]{1,0:T(8,128)(2,1)}, bf16[128,1792]{1,0:T(8,128)(2,1)}, u32[]{:S(2)}, u32[]{:S(2)}) collective-permute-start(bf16[128,1792]{1,0:T(8,128)(2,1)} %get-tuple-element.29), channel_id=1, source_target_pairs={{0,16},{8,24},{16,0},{24,8},{1,17},{9,25},{17,1},{25,9},{2,18},{10... | collective-permute-start | bytes 1376264 | tf_op jit(solution)/shard_map/ppermute | solution.py:24
  110.6 24.6 %collective-permute-start.9 = (bf16[128,1792]{1,0:T(8,128)(2,1)}, bf16[128,1792]{1,0:T(8,128)(2,1)}, u32[]{:S(2)}, u32[]{:S(2)}) collective-permute-start(bf16[128,1792]{1,0:T(8,128)(2,1)} %get-tuple-element.28), channel_id=1, source_target_pairs={{0,8},{8,0},{16,24},{24,16},{1,9},{9,1},{17,25},{25,17},{2,10},{10... | collective-permute-start | bytes 1376264 | tf_op jit(solution)/shard_map/ppermute | solution.py:24
  111.5 28.3 %collective-permute-start.36 = (bf16[128,1792]{1,0:T(8,128)(2,1)}, bf16[128,1792]{1,0:T(8,128)(2,1)}, u32[]{:S(2)}, u32[]{:S(2)}) collective-permute-start(bf16[128,1792]{1,0:T(8,128)(2,1)} %get-tuple-element.30), channel_id=1, source_target_pairs={{0,24},{8,16},{16,8},{24,0},{1,25},{9,17},{17,9},{25,1},{2,26},{10... | collective-permute-start | bytes 1376264 | tf_op jit(solution)/shard_map/ppermute | solution.py:24
  113.6 33.1 %collective-permute-start.37 = (bf16[128,1792]{1,0:T(8,128)(2,1)}, bf16[128,1792]{1,0:T(8,128)(2,1)}, u32[]{:S(2)}, u32[]{:S(2)}) collective-permute-start(bf16[128,1792]{1,0:T(8,128)(2,1)} %get-tuple-element.32), channel_id=1, source_target_pairs={{0,16},{8,24},{16,0},{24,8},{1,17},{9,25},{17,1},{25,9},{2,18},{10... | collective-permute-start | bytes 1376264 | tf_op jit(solution)/shard_map/ppermute | solution.py:24
  120.1 26.6 %collective-permute-start.38 = (bf16[128,1792]{1,0:T(8,128)(2,1)}, bf16[128,1792]{1,0:T(8,128)(2,1)}, u32[]{:S(2)}, u32[]{:S(2)}) collective-permute-start(bf16[128,1792]{1,0:T(8,128)(2,1)} %get-tuple-element.31), channel_id=1, source_target_pairs={{0,8},{8,0},{16,24},{24,16},{1,9},{9,1},{17,25},{25,17},{2,10},{10... | collective-permute-start | bytes 1376264 | tf_op jit(solution)/shard_map/ppermute | solution.py:24
  156.2 49.9 %collective-permute-start.16 = (bf16[128,1792]{1,0:T(8,128)(2,1)}, bf16[128,1792]{1,0:T(8,128)(2,1)}, u32[]{:S(2)}, u32[]{:S(2)}) collective-permute-start(bf16[128,1792]{1,0:T(8,128)(2,1)} %get-tuple-element.16), channel_id=1, source_target_pairs={{0,8},{8,0},{16,24},{24,16},{1,9},{9,1},{17,25},{25,17},{2,10},{10... | collective-permute-start | bytes 1376264 | tf_op jit(solution)/shard_map/ppermute | solution.py:24
  157.6 49.6 %collective-permute-start.17 = (bf16[128,1792]{1,0:T(8,128)(2,1)}, bf16[128,1792]{1,0:T(8,128)(2,1)}, u32[]{:S(2)}, u32[]{:S(2)}) collective-permute-start(bf16[128,1792]{1,0:T(8,128)(2,1)} %get-tuple-element.16), channel_id=1, source_target_pairs={{0,16},{8,24},{16,0},{24,8},{1,17},{9,25},{17,1},{25,9},{2,18},{10... | collective-permute-start | bytes 1376264 | tf_op jit(solution)/shard_map/ppermute | solution.py:24
  158.7 49.6 %collective-permute-start.18 = (bf16[128,1792]{1,0:T(8,128)(2,1)}, bf16[128,1792]{1,0:T(8,128)(2,1)}, u32[]{:S(2)}, u32[]{:S(2)}) collective-permute-start(bf16[128,1792]{1,0:T(8,128)(2,1)} %get-tuple-element.16), channel_id=1, source_target_pairs={{0,24},{8,16},{16,8},{24,0},{1,25},{9,17},{17,9},{25,1},{2,26},{10... | collective-permute-start | bytes 1376264 | tf_op jit(solution)/shard_map/ppermute | solution.py:24
  175.6 16.2 %collective-permute-start.47 = (bf16[64,1792]{1,0:T(8,128)(2,1)}, bf16[64,1792]{1,0:T(8,128)(2,1)S(1)}, u32[]{:S(2)}, u32[]{:S(2)}) collective-permute-start(bf16[64,1792]{1,0:T(8,128)(2,1)} %get-tuple-element.8), channel_id=1, source_target_pairs={{0,8},{8,0},{16,24},{24,16},{1,9},{9,1},{17,25},{25,17},{2,10},{10... | collective-permute-start | bytes 688136 | tf_op jit(solution)/shard_map/ppermute | solution.py:24
  225.3 14.8 %collective-permute-start.25 = (bf16[64,2048]{1,0:T(8,128)(2,1)S(1)}, bf16[64,2048]{1,0:T(8,128)(2,1)S(1)}, u32[]{:S(2)}, u32[]{:S(2)}) collective-permute-start(bf16[64,2048]{1,0:T(8,128)(2,1)S(1)} %get-tuple-element.21), channel_id=1, source_target_pairs={{0,1},{1,0},{2,3},{3,2},{4,5},{5,4},{6,7},{7,6},{8,9},{9,8},{10,11... | collective-permute-start | bytes 786440 | tf_op jit(solution)/shard_map/ppermute | solution.py:24
  235.2 22.1 %collective-permute-start.22 = (bf16[64,2048]{1,0:T(8,128)(2,1)S(1)}, bf16[64,2048]{1,0:T(8,128)(2,1)S(1)}, u32[]{:S(2)}, u32[]{:S(2)}) collective-permute-start(bf16[64,2048]{1,0:T(8,128)(2,1)S(1)} %get-tuple-element.19), channel_id=1, source_target_pairs={{0,4},{1,5},{2,6},{3,7},{4,0},{5,1},{6,2},{7,3},{8,12},{9,13},{10,... | collective-permute-start | bytes 786440 | tf_op jit(solution)/shard_map/ppermute | solution.py:24
  235.8 21.5 %collective-permute-start.24 = (bf16[64,2048]{1,0:T(8,128)(2,1)S(1)}, bf16[64,2048]{1,0:T(8,128)(2,1)S(1)}, u32[]{:S(2)}, u32[]{:S(2)}) collective-permute-start(bf16[64,2048]{1,0:T(8,128)(2,1)S(1)} %get-tuple-element.18), channel_id=1, source_target_pairs={{0,2},{1,3},{2,0},{3,1},{4,6},{5,7},{6,4},{7,5},{8,10},{9,11},{10,... | collective-permute-start | bytes 786440 | tf_op jit(solution)/shard_map/ppermute | solution.py:24
  (42 other events, 341.1 us)

commit v2 on v1

--- a/solution.py
+++ b/solution.py
@@ -28,38 +28,44 @@
     return lax.dynamic_slice_in_dim(x, index * count, count)
 
 
-def put(whole, x, index):
-    return lax.dynamic_update_slice_in_dim(whole, x, index * x.shape[0], 0)
-
-
-def gather_far(x, axis, step):
-    return {b: x if b == 0 else flip(x, axis, b) for b in range(0, lax.axis_size(axis), step)}
-
-
-def gather_tensor(x):
-    me = lax.axis_index("tensor")
-    held = gather_far(x, "tensor", 2)
-    whole = jnp.zeros((x.shape[0] * lax.axis_size("tensor"),) + x.shape[1:], x.dtype)
-    for b, block in held.items():
-        whole = put(whole, block, me ^ b)
-        whole = put(whole, flip(block, "tensor", 1), me ^ b ^ 1)
-    return whole
-
-
-def gather_dp(x):
-    me = lax.axis_index("dp")
-    whole = jnp.zeros((x.shape[0] * lax.axis_size("dp"),) + x.shape[1:], x.dtype)
-    for b, block in gather_far(x, "dp", 1).items():
-        whole = put(whole, block, me ^ b)
-    return whole
+def after(x, *done):
+    return lax.optimization_barrier((x,) + done)[0]
+
+
+def reorder(x, axis):
+    n = lax.axis_size(axis)
+    me = lax.axis_index(axis)
+    bits = 1
+    while bits < n:
+        half = x.shape[0] // n * bits
+        pieces = [x[i * half : (i + 1) * half] for i in range(n // bits)]
+        swapped = jnp.concatenate([pieces[i ^ 1] for i in range(n // bits)])
+        x = jnp.where((me // bits) % 2 == 1, swapped, x)
+        bits *= 2
+    return x
+
+
+def far_blocks(x, axis, step):
+    return [x if b == 0 else flip(x, axis, b) for b in range(0, lax.axis_size(axis), step)]
+
+
+def with_mates(far):
+    return jnp.concatenate([block for own in far for block in (own, flip(own, "tensor", 1))])
 
 
 def scatter_dp(x):
     n = lax.axis_size("dp")
     me = lax.axis_index("dp")
-    count = x.shape[0] // n
-    got = [flip(rows(x, me ^ b, count), "dp", b) for b in range(n - 1, 0, -1)]
-    total = rows(x, me, count).astype(jnp.float32)
+    mine = lax.axis_index("tensor")
+    size = lax.axis_size("tensor")
+    per = size // n
+    count = x.shape[0] // size
+
+    def group(g):
+        return jnp.concatenate([rows(x, (g * per + i) ^ mine, count) for i in range(per)])
+
+    got = [flip(group(me ^ b), "dp", b) for b in range(n - 1, 0, -1)]
+    total = group(me).astype(jnp.float32)
     for piece in got:
         total = total + piece.astype(jnp.float32)
     return total
@@ -68,11 +74,17 @@
 def scatter_tensor(x):
     n = lax.axis_size("tensor")
     me = lax.axis_index("tensor")
+    per = n // lax.axis_size("dp")
+    other = lax.axis_index("dp")
     count = x.shape[0] // n
+
+    def block(a):
+        return rows(x, ((a // per) ^ other) * per + a % per, count)
+
     total = None
     for b in range(n - 2, -1, -2):
-        mate = flip(rows(x, me ^ b ^ 1, count), "tensor", 1).astype(jnp.float32)
-        pair = rows(x, me ^ b, count).astype(jnp.float32) + mate
+        mate = flip(block(me ^ b ^ 1), "tensor", 1).astype(jnp.float32)
+        pair = block(me ^ b).astype(jnp.float32) + mate
         if b:
             pair = flip(pair.astype(x.dtype), "tensor", b).astype(jnp.float32)
         total = pair if total is None else total + pair
@@ -151,23 +163,33 @@
     group_tenants = pick(tenants, dp_index * blocks_group + arange(blocks_group))
     input_tenants = pick(tenants, tensor_index * blocks_in + arange(blocks_in))
     block_slots = pick(owners, tenants)
-    mask_all = mask_of(tenants, 0, tenant_count)
+    near = arange(blocks_all)
+    near = ((near // blocks_in) ^ tensor_index) * blocks_in + near % blocks_in
+    across = arange(blocks_all)
+    across = ((across // blocks_group) ^ dp_index) * blocks_group + across % blocks_group
+    near_tenants = pick(tenants, near)
+    across_tenants = pick(tenants, across)
+    across_slots = pick(block_slots, across)
+    mask_near = mask_of(near_tenants, 0, tenant_count)
+    mask_across = mask_of(across_tenants, 0, tenant_count)
     mask_group = mask_of(group_tenants, 0, tenant_count)
     mask_input = mask_of(input_tenants, 0, tenant_count)
-    mask_held = mask_of(tenants, tensor_index * tenants_here, tenants_here)
-    mask_slots = mask_of(block_slots, dp_index * slots_here, slots_here)
+    mask_held = mask_of(near_tenants, tensor_index * tenants_here, tenants_here)
+    mask_slots = mask_of(across_slots, dp_index * slots_here, slots_here)
     mask_local = mask_of(arange(blocks_group), 0, blocks_group)
     gate_raise = gate_out.reshape(columns, width_here)
     up_raise = up_out.reshape(columns, width_here)
     down_raise = down_out.reshape(columns, feat_here)
 
-    all_inputs = gather_tensor(tokens)
-    all_cot = gather_tensor(cotangent)
+    far_tokens = far_blocks(tokens, "tensor", 2)
+    all_inputs = with_mates(far_tokens)
+    far_cot = far_blocks(after(cotangent, *far_tokens), "tensor", 2)
+    all_cot = with_mates(far_cot)
 
     gate_sum = scatter_dp(dot(all_inputs, gate_weight).astype(bf16))
     rank_parts = jnp.concatenate(
         [
-            collapse(dot(all_inputs, as_rows(table), 1, 1).astype(bf16), mask_all)
+            collapse(dot(all_inputs, as_rows(table), 1, 1).astype(bf16), mask_near)
             for table in (gate_in, up_in)
         ],
         axis=1,
@@ -179,23 +201,29 @@
     gate_full = gate_sum + adapter_scale * dot(expand(gate_rank, mask_group), gate_raise)
     up_full = up_sum + adapter_scale * dot(expand(up_rank, mask_group), up_raise)
     hidden = (jax.nn.silu(gate_full) * up_full).astype(bf16)
-    all_hidden = gather_dp(hidden)
-
-    down_back = adapter_scale * collapse(dot(all_cot, down_raise, 1, 1), mask_all)
-    down_back = sum_all(down_back, "dp").astype(bf16)
+    far_hidden = far_blocks(hidden, "dp", 1)
+    all_hidden = jnp.concatenate(far_hidden)
+
+    down_back = adapter_scale * collapse(dot(all_cot, down_raise, 1, 1), mask_near)
+    down_back = reorder(sum_all(down_back, "dp"), "tensor").astype(bf16)
     group_down_back = rows(down_back, dp_index, group_rows)
     down_drop = as_rows(down_in)
-    hidden_grad = scatter_dp(dot(all_cot, down_weight, 1, 1).astype(bf16))
+    hidden_grad_part = dot(all_cot, down_weight, 1, 1).astype(bf16)
+    hidden_grad = scatter_dp(after(hidden_grad_part, *far_hidden))
     hidden_grad = hidden_grad + dot(expand(group_down_back, mask_group), down_drop)
 
-    out_sum = scatter_tensor(dot(all_hidden, down_weight).astype(bf16))
-    down_rank = collapse(dot(all_hidden, down_drop, 1, 1).astype(bf16), mask_all)
-    down_rank = sum_all(down_rank, "tensor").astype(bf16)
+    out_part = dot(all_hidden, down_weight).astype(bf16)
+    out_sum = scatter_tensor(out_part)
+    hidden_grad = after(hidden_grad, out_part)
+    down_rank = collapse(dot(all_hidden, down_drop, 1, 1).astype(bf16), mask_across)
+    down_rank = reorder(sum_all(down_rank, "tensor"), "dp").astype(bf16)
     own_down_rank = rows(down_rank, tensor_index, rows_in)
     mixed = (
         out_sum + adapter_scale * dot(expand(own_down_rank, mask_input), down_raise)
     ).astype(bf16)
-    grad_down_out = adapter_scale * dot(expand(down_rank, mask_held), all_cot, 0, 0)
+    grad_down_out = adapter_scale * dot(
+        expand(reorder(down_rank, "tensor"), mask_held), all_cot, 0, 0
+    )
     grad_down_out = grad_down_out.reshape(tenants_here, rank, feat_here)
 
     sig = jax.nn.sigmoid(gate_full)
@@ -208,7 +236,9 @@
         ],
         axis=1,
     )
-    backs = gather_dp(sum_all(backs, "tensor").astype(bf16))
+    backs = sum_all(backs, "tensor").astype(bf16)
+    backs = jnp.concatenate(far_blocks(backs, "dp", 1))
+    backs = reorder(reorder(backs, "dp"), "tensor")
 
     lifts = adapter_scale * jnp.concatenate(
         [
@@ -217,12 +247,12 @@
         ],
         axis=0,
     )
-    lifts = gather_dp(lifts.astype(bf16))
+    lifts = jnp.concatenate(far_blocks(lifts.astype(bf16), "dp", 1))
 
     def own_lift(which):
         shape = (slots_here, rank, dp_count, 2, blocks_group, rank)
         iota = lambda axis: lax.broadcasted_iota(jnp.int32, shape, axis)
-        slots = block_slots.reshape(1, 1, dp_count, 1, blocks_group, 1)
+        slots = across_slots.reshape(1, 1, dp_count, 1, blocks_group, 1)
         chosen = (
             (iota(0) + dp_index * slots_here == slots) & (iota(1) == iota(5)) & (iota(3) == which)
         )
@@ -238,7 +268,7 @@
 
     grad_gate_in = own_in(backs[:, :rank], mask_held, all_inputs, tenants_here)
     grad_up_in = own_in(backs[:, rank:], mask_held, all_inputs, tenants_here)
-    grad_down_in = own_in(down_back, mask_slots, all_hidden, slots_here)
+    grad_down_in = own_in(reorder(down_back, "dp"), mask_slots, all_hidden, slots_here)
     return (
         mixed,
         grad_gate_in,

time: 262 us -> 242 us (0.924)
  starting transfers between devices: 60.4 us -> 46.5 us
  local copies, waits for them, and re-layouts: 36.1 us -> 22.5 us
  waiting for transfers between devices: 88.3 us -> 76.6 us
  other arithmetic: 13.3 us -> 24.3 us
  matrix products: 60.9 us -> 69.5 us
    dynamic_update_slice x25 -> x0, local copies, waits for them, and re-layouts: 21.7 us -> none  [put(): return lax.dynamic_update_slice_in_dim(whole, x, index * x.shape[0], 0)]
    ppermute x50, starting transfers between devices: 60.4 us -> 46.5 us  [flip(): return lax.ppermute(x, axis, [(i, i ^ bits) for i in range(n)])]
    ppermute x50, waiting for transfers between devices: 88.3 us -> 76.6 us  [flip(): return lax.ppermute(x, axis, [(i, i ^ bits) for i in range(n)])]
    concatenate x0 -> x12, other arithmetic: none -> 10.6 us  [group(): jnp.concatenate([rows(x, g * per + i ^ mine, count) for i in range(per)])]
    dot_general x25, matrix products: 60.9 us -> 69.5 us  [dot(): lax.dot_general(a, b, (((ca,), (cb,)), ((), ())), preferred_element_type=...]
    unnamed x48 -> x74, local copies, waits for them, and re-layouts: 4.95 us -> 11.2 us
    dynamic_update_slice x3 -> x0, other arithmetic: 2.81 us -> none  [put(): return lax.dynamic_update_slice_in_dim(whole, x, index * x.shape[0], 0)]
  transfers between devices with their start and end apart: 50 -> 50, of which waited for: 15 -> 15; matrix products, arithmetic and copies ran while one was open for 36% -> 41% of each run, Pallas kernels for 0% -> 0%
where the time goes in v2:
time: 242 us; the launch traced here: 241 us
  waiting for transfers between devices  76.6 us (32%)
  matrix products  69.5 us (29%)
  starting transfers between devices  46.5 us (19%)
  other arithmetic  24.3 us (10%)
  local copies, waits for them, and re-layouts  22.5 us (9%)
    ppermute x50, waiting for transfers between devices, flip(): return lax.ppermute(x, axis, [(i, i ^ bits) for i in range(n)])  76.6 us
    dot_general x25, matrix products, dot(): lax.dot_general(a, b, (((ca,), (cb,)), ((), ())), preferred_element_type=...  69.5 us
    ppermute x50, starting transfers between devices, flip(): return lax.ppermute(x, axis, [(i, i ^ bits) for i in range(n)])  46.5 us
    unnamed x74, local copies, waits for them, and re-layouts  11.2 us
    concatenate x12, other arithmetic, group(): jnp.concatenate([rows(x, g * per + i ^ mine, count) for i in range(per)])  10.6 us
    dynamic_slice x4, local copies, waits for them, and re-layouts, rows(): return lax.dynamic_slice_in_dim(x, index * count, count)  5.49 us
  transfers between devices with their start and end apart: 50, of which 15 were waited for; matrix products, arithmetic and copies ran while one was open for 41% of the time, Pallas kernels for 0%

profile of v2, /device:TPU:0, one launch (start us, length us, event | category | flops | bytes accessed | tf_op | source)
XLA Modules:
  0.0 240.8 jit_solution(13709380135621110615)
XLA Ops:
  0.6 5.1 %collective-permute-start.5 = (bf16[64,2048]{1,0:T(8,128)(2,1)}, bf16[64,2048]{1,0:T(8,128)(2,1)S(1)}, u32[]{:S(2)}, u32[]{:S(2)}) collective-permute-start(bf16[64,2048]{1,0:T(8,128)(2,1)} %param.13), channel_id=1, source_target_pairs={{0,6},{1,7},{2,4},{3,5},{4,2},{5,3},{6,0},{7,1},{8,14},{9,15},{10,... | collective-permute-start | bytes 786440 | tf_op jit(solution)/shard_map/ppermute | solution.py:24
  18.9 9.5 %collective-permute-done.3 = bf16[64,2048]{1,0:T(8,128)(2,1)} collective-permute-done((bf16[64,2048]{1,0:T(8,128)(2,1)}, bf16[64,2048]{1,0:T(8,128)(2,1)}, u32[]{:S(2)}, u32[]{:S(2)}) %collective-permute-start.3) | collective-permute-done | bytes 262176 | tf_op jit(solution)/shard_map/ppermute | solution.py:24
  28.4 3.0 %collective-permute-start.30 = (bf16[64,2048]{1,0:T(8,128)(2,1)}, bf16[64,2048]{1,0:T(8,128)(2,1)}, u32[]{:S(2)}, u32[]{:S(2)}) collective-permute-start(bf16[64,2048]{1,0:T(8,128)(2,1)} %param.14), channel_id=1, source_target_pairs={{0,2},{1,3},{2,0},{3,1},{4,6},{5,7},{6,4},{7,5},{8,10},{9,11},{10,... | collective-permute-start | bytes 786440 | tf_op jit(solution)/shard_map/ppermute | solution.py:24
  37.6 2.2 fusion.18
  39.8 2.2 fusion.19
  45.3 7.0 %convolution_convert_fusion.2 = bf16[512,1792]{1,0:T(8,128)(2,1)S(1)} fusion(bf16[512,2048]{1,0:T(8,128)(2,1)S(1)} %constant_dynamic-update-slice_fusion, bf16[2048,1792]{1,0:T(8,128)(2,1)} %param.16), kind=kOutput, calls=%fused_computation.2 | convolution fusion | flops 3759013888 | bytes 11272192 | tf_op jit(solution)/shard_map/dot_general | solution.py:13
  53.3 7.1 %convolution_convert_fusion.3 = bf16[512,1792]{1,0:T(8,128)(2,1)S(1)} fusion(bf16[512,2048]{1,0:T(8,128)(2,1)S(1)} %constant_dynamic-update-slice_fusion, bf16[2048,1792]{1,0:T(8,128)(2,1)} %param.15), kind=kOutput, calls=%fused_computation.3 | convolution fusion | flops 3759013888 | bytes 11272192 | tf_op jit(solution)/shard_map/dot_general | solution.py:13
  70.2 2.5 %collective-permute-start.13 = (bf16[128,1792]{1,0:T(8,128)(2,1)}, bf16[128,1792]{1,0:T(8,128)(2,1)}, u32[]{:S(2)}, u32[]{:S(2)}) collective-permute-start(bf16[128,1792]{1,0:T(8,128)(2,1)} %pad_maximum_fusion.4), channel_id=1, source_target_pairs={{0,24},{8,16},{16,8},{24,0},{1,25},{9,17},{17,9},{25,1},{2,26},{10... | collective-permute-start | bytes 1376264 | tf_op jit(solution)/shard_map/ppermute | solution.py:24
  74.8 4.6 %collective-permute-done.34 = bf16[64,2048]{1,0:T(8,128)(2,1)S(1)} collective-permute-done((bf16[64,2048]{1,0:T(8,128)(2,1)S(1)}, bf16[64,2048]{1,0:T(8,128)(2,1)S(1)}, u32[]{:S(2)}, u32[]{:S(2)}) %collective-permute-start.34) | collective-permute-done | bytes 262176 | tf_op jit(solution)/shard_map/ppermute | solution.py:24
  79.4 2.5 %collective-permute-start.7 = (bf16[128,1792]{1,0:T(8,128)(2,1)}, bf16[128,1792]{1,0:T(8,128)(2,1)}, u32[]{:S(2)}, u32[]{:S(2)}) collective-permute-start(bf16[128,1792]{1,0:T(8,128)(2,1)} %pad_maximum_fusion.1), channel_id=1, source_target_pairs={{0,24},{8,16},{16,8},{24,0},{1,25},{9,17},{17,9},{25,1},{2,26},{10... | collective-permute-start | bytes 1376264 | tf_op jit(solution)/shard_map/ppermute | solution.py:24
  85.9 2.5 %convolution_multiply_fusion = f32[128,1792]{1,0:T(8,128)} fusion(bf16[256,1792]{1,0:T(8,128)(2,1)} %bitcast.58, s32[256]{0:T(256)S(1)} %get-tuple-element.123, s32[256]{0:T(256)S(1)} %get-tuple-element.126, s32[128]{0:T(128)S(1)} %eq.326, pred[256]{0:T(512)(128)(4,1)S(1)} %get-tuple-element.120, s32[256]{0:T(256)S(1)} %get-tuple-element.124, ...), kind=kOutput, calls=%fused_computation.4 | convolution fusion | flops 118857728 | bytes 1844736 | tf_op jit(solution)/shard_map/dot_general | solution.py:13
  88.4 16.0 %collective-permute-done.39 = f32[512,16]{0,1:T(8,128)S(1)} collective-permute-done((f32[512,16]{0,1:T(8,128)S(1)}, f32[512,16]{0,1:T(8,128)S(1)}, u32[]{:S(2)}, u32[]{:S(2)}) %collective-permute-start.39) | collective-permute-done | bytes 32800 | tf_op jit(solution)/shard_map/ppermute | solution.py:24
  104.9 8.9 %convolution_convert_fusion = bf16[512,1792]{1,0:T(8,128)(2,1)} fusion(bf16[512,2048]{1,0:T(8,128)(2,1)} %copy-done.5, bf16[1792,2048]{1,0:T(8,128)(2,1)} %param.17), kind=kOutput, calls=%fused_computation | convolution fusion | flops 3759013888 | bytes 11272192 | tf_op jit(solution)/shard_map/dot_general | solution.py:13
  117.2 8.6 %collective-permute-done.8 = bf16[128,1792]{1,0:T(8,128)(2,1)} collective-permute-done((bf16[128,1792]{1,0:T(8,128)(2,1)}, bf16[128,1792]{1,0:T(8,128)(2,1)}, u32[]{:S(2)}, u32[]{:S(2)}) %collective-permute-start.8) | collective-permute-done | bytes 458784 | tf_op jit(solution)/shard_map/ppermute | solution.py:24
  127.3 4.5 %multiply_convert_fusion.2 = (bf16[128,1792]{1,0:T(8,128)(2,1)}, f32[128,1792]{1,0:T(8,128)}) fusion(f32[128,1792]{1,0:T(8,128)} %convolution_multiply_fusion, bf16[128,1792]{1,0:T(8,128)(2,1)} %collective-permute-done.15, bf16[128,1792]{1,0:T(8,128)(2,1)} %collective-permute-done.14, bf16[128,1792]{1,0:T(8,128)(2,1)} %collective-permute-done.13, ...), kind=kOutput, calls=%fused_computation.54 | convolution fusion | flops 125280256 | bytes 6891008 | tf_op jit(solution)/shard_map/dot_general | solution.py:13
  135.3 11.1 %collective-permute-done.18 = bf16[128,1792]{1,0:T(8,128)(2,1)S(1)} collective-permute-done((bf16[128,1792]{1,0:T(8,128)(2,1)}, bf16[128,1792]{1,0:T(8,128)(2,1)S(1)}, u32[]{:S(2)}, u32[]{:S(2)}) %collective-permute-start.18) | collective-permute-done | bytes 458784 | tf_op jit(solution)/shard_map/ppermute | solution.py:24
  146.4 6.8 %collective-permute-done.17 = bf16[128,1792]{1,0:T(8,128)(2,1)S(1)} collective-permute-done((bf16[128,1792]{1,0:T(8,128)(2,1)}, bf16[128,1792]{1,0:T(8,128)(2,1)S(1)}, u32[]{:S(2)}, u32[]{:S(2)}) %collective-permute-start.17) | collective-permute-done | bytes 458784 | tf_op jit(solution)/shard_map/ppermute | solution.py:24
  154.0 2.7 %constant_dynamic-slice_fusion.8 = (bf16[64,1792]{1,0:T(8,128)(2,1)}, bf16[64,1792]{1,0:T(8,128)(2,1)S(1)}, bf16[64,1792]{1,0:T(8,128)(2,1)}, bf16[64,1792]{1,0:...) fusion(bf16[512,1792]{1,0:T(8,128)(2,1)} %convolution_convert_f, ...), kind=kLoop, calls=%fused_computation.224 | loop fusion | bytes 3670048 | tf_op jit(solution)/shard_map/dynamic_slice | solution.py:28
  156.7 2.6 %fusion.1 = f32[512,16]{0,1:T(8,128)S(1)} fusion(bf16[256,1792]{1,0:T(8,128)(2,1)} %bitcast.62, s32[512]{0:T(512)S(1)} %copy-done.13, s32[256]{0:T(256)S(1)} %get-tuple-element.123, s32[256]{0:T(256)S(1)} %get-tuple-element.126, pred[256]{0:T(512)(128)(4,1)S(1)} %get-tuple-element.120, s32[256]{0:T(256)S(1)} %get-tuple-element.124, ...), kind=kOutput, calls=%fused_computation.14 | convolution fusion | flops 481828864 | bytes 2791936 | tf_op jit(solution)/shard_map/dot_general | solution.py:13
  168.5 7.2 %convolution_convert_fusion.1 = bf16[512,2048]{1,0:T(8,128)(2,1)S(1)} fusion(bf16[1792,2048]{1,0:T(8,128)(2,1)} %param.17, bf16[128,1792]{1,0:T(8,128)(2,1)S(1)} %copy-done.20, bf16[128,1792]{1,0:T(8,128)(2,1)S(1)} %copy-done.22, bf16[128,1792]{1,0:T(8,128)(2,1)} %collective-permute-done.16, bf16[128,1792]{1,0:T(8,128)(2,1)S(1)} %copy-done.18), kind=kOutput, calls=%fused_computation.1 | convolution fusion | flops 3766484992 | bytes 11272192 | tf_op jit(solution)/shard_map/dot_general | solution.py:13
  180.9 2.8 %fusion.10 = f32[64,1792]{1,0:T(8,128)} fusion(s32[]{:T(128)S(6)} %mul.269, s32[64]{0:T(128)S(1)} %copy-done.26, s32[64]{0:T(128)S(1)} %copy-done.25, s32[512]{0:T(512)S(1)} %copy-done.12, pred[64]{0:T(512)(128)(4,1)S(1)} %copy-done.29, bf16[512,16]{0,1:T(8,128)(2,1)S(1)} %maximum_select_fusion.12, bf16[256,16]{0,1:T(8,128)(2,1)S(1)} %get-tuple-element.76, ...), kind=kOutput, calls=%fused_computation.29 | convolution fusion | flops 126035968 | bytes 2329733 | tf_op jit(solution)/shard_map/dot_general | solution.py:13
  184.9 2.9 %convolution_multiply_fusion.3 = f32[32,2048]{1,0:T(8,128)} fusion(bf16[512,2048]{1,0:T(8,128)(2,1)} %copy-done.5, s32[]{:T(128)S(6)} %mul.255, s32[32]{0:T(128)S(1)} %get-tuple-element.127, s32[32]{0:T(128)S(1)} %get-tuple-element.130, s32[512]{0:T(512)S(1)} %eq.333, pred[32]{0:T(512)(128)(4,1)S(1)} %get-tuple-element.118, ...), kind=kOutput, calls=%fused_computation.7 | convolution fusion | flops 67822592 | bytes 2394693 | tf_op jit(solution)/shard_map/dot_general | solution.py:13
  188.4 3.0 %add_add_fusion = f32[128,1792]{1,0:T(8,128)} fusion(bf16[128,1792]{1,0:T(8,128)(2,1)} %collective-permute-done.38, bf16[128,1792]{1,0:T(8,128)(2,1)} %collective-permute-done.37, bf16[128,1792]{1,0:T(8,128)(2,1)} %collective-permute-done.36, bf16[64,1792]{1,0:T(8,128)(2,1)} %get-tuple-element.34, bf16[64,1792]{1,0:T(8,128)(2,1)S(1)} %copy-done.8, ...), kind=kOutput, calls=%fused_computation.53 | convolution fusion | flops 121151488 | bytes 3679748 | tf_op jit(solution)/shard_map/dot_general | solution.py:13
  191.5 3.0 %multiply_convert_fusion.1 = (bf16[128,1792]{1,0:T(8,128)(2,1)S(1)}, bf16[128,1792]{1,0:T(8,128)(2,1)S(1)}) fusion(f32[128,1792]{1,0:T(8,128)} %get-tuple-element.17, f32[128,1792]{1,0:T(8,128)} %add_add_fusion, f32[128,1792]{1,0:T(8,128)} %convolution_multiply_fusion, bf16[128,1792]{1,0:T(8,128)(2,1)} %collective-permute-done.15, ...), kind=kLoop, calls=%fused_computation.52 | loop fusion | flops 5505024 | bytes 5505024 | tf_op jit(solution)/shard_map/convert_element_type | solution.py:231
  196.5 2.3 add_convert_fusion.3
  198.9 2.5 %collective-permute-start.20 = (bf16[64,2048]{1,0:T(8,128)(2,1)}, bf16[64,2048]{1,0:T(8,128)(2,1)}, u32[]{:S(2)}, u32[]{:S(2)}) collective-permute-start(bf16[64,2048]{1,0:T(8,128)(2,1)} %get-tuple-element.18), channel_id=1, source_target_pairs={{0,6},{1,7},{2,4},{3,5},{4,2},{5,3},{6,0},{7,1},{8,14},{9,15},{10,... | collective-permute-start | bytes 786440 | tf_op jit(solution)/shard_map/ppermute | solution.py:24
  202.8 6.8 %collective-permute-done.42 = f32[128,32]{0,1:T(8,128)S(1)} collective-permute-done((f32[128,32]{0,1:T(8,128)S(1)}, f32[128,32]{0,1:T(8,128)S(1)}, u32[]{:S(2)}, u32[]{:S(2)}) %collective-permute-start.42) | collective-permute-done | bytes 16416 | tf_op jit(solution)/shard_map/ppermute | solution.py:24
  210.2 2.1 fusion.22
  228.2 3.0 %collective-permute-done.24 = bf16[64,2048]{1,0:T(8,128)(2,1)} collective-permute-done((bf16[64,2048]{1,0:T(8,128)(2,1)}, bf16[64,2048]{1,0:T(8,128)(2,1)}, u32[]{:S(2)}, u32[]{:S(2)}) %collective-permute-start.24) | collective-permute-done | bytes 262176 | tf_op jit(solution)/shard_map/ppermute | solution.py:24
  233.2 3.2 %add_convert_fusion = bf16[64,2048]{1,0:T(8,128)(2,1)} fusion(bf16[64,2048]{1,0:T(8,128)(2,1)} %collective-permute-done.25, bf16[64,2048]{1,0:T(8,128)(2,1)} %collective-permute-done.24, bf16[64,2048]{1,0:T(8,128)(2,1)} %collective-permute-done.22, bf16[64,2048]{1,0:T(8,128)(2,1)} %collective-permute-done.20, bf16[512,2048]{1,0:T(8,128)(2,1)} %copy-done.6, ...), kind=kOutput, calls=%fused_computation.60 | convolution fusion | flops 69279744 | bytes 2630668 | tf_op jit(solution)/shard_map/dot_general | solution.py:13
  236.5 2.1 fusion.25
  238.6 2.1 fusion.26
  (267 shorter events, 86.6 us)
Async XLA Ops:
  0.6 18.2 %collective-permute-start.5 = (bf16[64,2048]{1,0:T(8,128)(2,1)}, bf16[64,2048]{1,0:T(8,128)(2,1)S(1)}, u32[]{:S(2)}, u32[]{:S(2)}) collective-permute-start(bf16[64,2048]{1,0:T(8,128)(2,1)} %param.13), channel_id=1, source_target_pairs={{0,6},{1,7},{2,4},{3,5},{4,2},{5,3},{6,0},{7,1},{8,14},{9,15},{10,... | collective-permute-start | bytes 786440 | tf_op jit(solution)/shard_map/ppermute | solution.py:24
  5.8 22.6 %collective-permute-start.3 = (bf16[64,2048]{1,0:T(8,128)(2,1)}, bf16[64,2048]{1,0:T(8,128)(2,1)}, u32[]{:S(2)}, u32[]{:S(2)}) collective-permute-start(bf16[64,2048]{1,0:T(8,128)(2,1)} %param.13), channel_id=1, source_target_pairs={{0,4},{1,5},{2,6},{3,7},{4,0},{5,1},{6,2},{7,3},{8,12},{9,13},{10,... | collective-permute-start | bytes 786440 | tf_op jit(solution)/shard_map/ppermute | solution.py:24
  5.8 22.6 %collective-permute-start.1 = (bf16[64,2048]{1,0:T(8,128)(2,1)}, bf16[64,2048]{1,0:T(8,128)(2,1)}, u32[]{:S(2)}, u32[]{:S(2)}) collective-permute-start(bf16[64,2048]{1,0:T(8,128)(2,1)} %param.13), channel_id=1, source_target_pairs={{0,2},{1,3},{2,0},{3,1},{4,6},{5,7},{6,4},{7,5},{8,10},{9,11},{10,... | collective-permute-start | bytes 786440 | tf_op jit(solution)/shard_map/ppermute | solution.py:24
  6.4 27.2 %collective-permute-start = (bf16[64,2048]{1,0:T(8,128)(2,1)}, bf16[64,2048]{1,0:T(8,128)(2,1)}, u32[]{:S(2)}, u32[]{:S(2)}) collective-permute-start(bf16[64,2048]{1,0:T(8,128)(2,1)} %param.13), channel_id=1, source_target_pairs={{0,1},{1,0},{2,3},{3,2},{4,5},{5,4},{6,7},{7,6},{8,9},{9,8},{10,11... | collective-permute-start | bytes 786440 | tf_op jit(solution)/shard_map/ppermute | solution.py:24
  28.4 44.8 %collective-permute-start.32 = (bf16[64,2048]{1,0:T(8,128)(2,1)}, bf16[64,2048]{1,0:T(8,128)(2,1)}, u32[]{:S(2)}, u32[]{:S(2)}) collective-permute-start(bf16[64,2048]{1,0:T(8,128)(2,1)} %param.14), channel_id=1, source_target_pairs={{0,4},{1,5},{2,6},{3,7},{4,0},{5,1},{6,2},{7,3},{8,12},{9,13},{10,... | collective-permute-start | bytes 786440 | tf_op jit(solution)/shard_map/ppermute | solution.py:24
  28.4 37.8 %collective-permute-start.30 = (bf16[64,2048]{1,0:T(8,128)(2,1)}, bf16[64,2048]{1,0:T(8,128)(2,1)}, u32[]{:S(2)}, u32[]{:S(2)}) collective-permute-start(bf16[64,2048]{1,0:T(8,128)(2,1)} %param.14), channel_id=1, source_target_pairs={{0,2},{1,3},{2,0},{3,1},{4,6},{5,7},{6,4},{7,5},{8,10},{9,11},{10,... | collective-permute-start | bytes 786440 | tf_op jit(solution)/shard_map/ppermute | solution.py:24
  31.4 35.3 %collective-permute-start.29 = (bf16[64,2048]{1,0:T(8,128)(2,1)}, bf16[64,2048]{1,0:T(8,128)(2,1)}, u32[]{:S(2)}, u32[]{:S(2)}) collective-permute-start(bf16[64,2048]{1,0:T(8,128)(2,1)} %param.14), channel_id=1, source_target_pairs={{0,1},{1,0},{2,3},{3,2},{4,5},{5,4},{6,7},{7,6},{8,9},{9,8},{10,11... | collective-permute-start | bytes 786440 | tf_op jit(solution)/shard_map/ppermute | solution.py:24
  42.2 26.5 %collective-permute-start.11 = (bf16[128,32]{0,1:T(8,128)(2,1)S(1)}, bf16[128,32]{0,1:T(8,128)(2,1)S(1)}, u32[]{:S(2)}, u32[]{:S(2)}) collective-permute-start(bf16[128,32]{0,1:T(8,128)(2,1)S(1)} %pad_maximum_fusion.11), channel_id=1, source_target_pairs={{0,16},{8,24},{16,0},{24,8},{1,17},{9,25},{17,1},{25,9},{2,18},{10... | collective-permute-start | bytes 24584 | tf_op jit(solution)/shard_map/ppermute | solution.py:24
  43.9 26.3 %collective-permute-start.10 = (bf16[128,32]{0,1:T(8,128)(2,1)S(1)}, bf16[128,32]{0,1:T(8,128)(2,1)S(1)}, u32[]{:S(2)}, u32[]{:S(2)}) collective-permute-start(bf16[128,32]{0,1:T(8,128)(2,1)S(1)} %pad_maximum_fusion.10), channel_id=1, source_target_pairs={{0,24},{8,16},{16,8},{24,0},{1,25},{9,17},{17,9},{25,1},{2,26},{10... | collective-permute-start | bytes 24584 | tf_op jit(solution)/shard_map/ppermute | solution.py:24
  68.7 10.7 %collective-permute-start.34 = (bf16[64,2048]{1,0:T(8,128)(2,1)S(1)}, bf16[64,2048]{1,0:T(8,128)(2,1)S(1)}, u32[]{:S(2)}, u32[]{:S(2)}) collective-permute-start(bf16[64,2048]{1,0:T(8,128)(2,1)S(1)} %copy-done.10), channel_id=1, source_target_pairs={{0,6},{1,7},{2,4},{3,5},{4,2},{5,3},{6,0},{7,1},{8,14},{9,15},{10,... | collective-permute-start | bytes 786440 | tf_op jit(solution)/shard_map/ppermute | solution.py:24
  70.2 45.4 %collective-permute-start.13 = (bf16[128,1792]{1,0:T(8,128)(2,1)}, bf16[128,1792]{1,0:T(8,128)(2,1)}, u32[]{:S(2)}, u32[]{:S(2)}) collective-permute-start(bf16[128,1792]{1,0:T(8,128)(2,1)} %pad_maximum_fusion.4), channel_id=1, source_target_pairs={{0,24},{8,16},{16,8},{24,0},{1,25},{9,17},{17,9},{25,1},{2,26},{10... | collective-permute-start | bytes 1376264 | tf_op jit(solution)/shard_map/ppermute | solution.py:24
  72.6 44.6 %collective-permute-start.14 = (bf16[128,1792]{1,0:T(8,128)(2,1)}, bf16[128,1792]{1,0:T(8,128)(2,1)}, u32[]{:S(2)}, u32[]{:S(2)}) collective-permute-start(bf16[128,1792]{1,0:T(8,128)(2,1)} %pad_maximum_fusion.5), channel_id=1, source_target_pairs={{0,16},{8,24},{16,0},{24,8},{1,17},{9,25},{17,1},{25,9},{2,18},{10... | collective-permute-start | bytes 1376264 | tf_op jit(solution)/shard_map/ppermute | solution.py:24
  73.2 44.0 %collective-permute-start.15 = (bf16[128,1792]{1,0:T(8,128)(2,1)}, bf16[128,1792]{1,0:T(8,128)(2,1)}, u32[]{:S(2)}, u32[]{:S(2)}) collective-permute-start(bf16[128,1792]{1,0:T(8,128)(2,1)} %pad_maximum_fusion.6), channel_id=1, source_target_pairs={{0,8},{8,0},{16,24},{24,16},{1,9},{9,1},{17,25},{25,17},{2,10},{10... | collective-permute-start | bytes 1376264 | tf_op jit(solution)/shard_map/ppermute | solution.py:24
  79.4 37.8 %collective-permute-start.7 = (bf16[128,1792]{1,0:T(8,128)(2,1)}, bf16[128,1792]{1,0:T(8,128)(2,1)}, u32[]{:S(2)}, u32[]{:S(2)}) collective-permute-start(bf16[128,1792]{1,0:T(8,128)(2,1)} %pad_maximum_fusion.1), channel_id=1, source_target_pairs={{0,24},{8,16},{16,8},{24,0},{1,25},{9,17},{17,9},{25,1},{2,26},{10... | collective-permute-start | bytes 1376264 | tf_op jit(solution)/shard_map/ppermute | solution.py:24
  85.3 19.1 %collective-permute-start.39 = (f32[512,16]{0,1:T(8,128)S(1)}, f32[512,16]{0,1:T(8,128)S(1)}, u32[]{:S(2)}, u32[]{:S(2)}) collective-permute-start(f32[512,16]{0,1:T(8,128)S(1)} %convolution_multiply_fusion.4), channel_id=1, source_target_pairs={{0,8},{8,0},{16,24},{24,16},{1,9},{9,1},{17,25},{25,17},{2,10},{10... | collective-permute-start | bytes 98312 | tf_op jit(solution)/shard_map/ppermute | solution.py:24
  104.4 9.4 %collective-permute-start.40 = (f32[512,16]{0,1:T(8,128)S(1)}, f32[512,16]{0,1:T(8,128)S(1)}, u32[]{:S(2)}, u32[]{:S(2)}) collective-permute-start(f32[512,16]{0,1:T(8,128)S(1)} %add.507), channel_id=1, source_target_pairs={{0,16},{8,24},{16,0},{24,8},{1,17},{9,25},{17,1},{25,9},{2,18},{10... | collective-permute-start | bytes 98312 | tf_op jit(solution)/shard_map/ppermute | solution.py:24
  113.8 12.0 %collective-permute-start.8 = (bf16[128,1792]{1,0:T(8,128)(2,1)}, bf16[128,1792]{1,0:T(8,128)(2,1)}, u32[]{:S(2)}, u32[]{:S(2)}) collective-permute-start(bf16[128,1792]{1,0:T(8,128)(2,1)} %pad_maximum_fusion.2), channel_id=1, source_target_pairs={{0,16},{8,24},{16,0},{24,8},{1,17},{9,25},{17,1},{25,9},{2,18},{10... | collective-permute-start | bytes 1376264 | tf_op jit(solution)/shard_map/ppermute | solution.py:24
  115.6 11.8 %collective-permute-start.9 = (bf16[128,1792]{1,0:T(8,128)(2,1)}, bf16[128,1792]{1,0:T(8,128)(2,1)}, u32[]{:S(2)}, u32[]{:S(2)}) collective-permute-start(bf16[128,1792]{1,0:T(8,128)(2,1)} %pad_maximum_fusion.3), channel_id=1, source_target_pairs={{0,8},{8,0},{16,24},{24,16},{1,9},{9,1},{17,25},{25,17},{2,10},{10... | collective-permute-start | bytes 1376264 | tf_op jit(solution)/shard_map/ppermute | solution.py:24
  131.8 14.6 %collective-permute-start.18 = (bf16[128,1792]{1,0:T(8,128)(2,1)}, bf16[128,1792]{1,0:T(8,128)(2,1)S(1)}, u32[]{:S(2)}, u32[]{:S(2)}) collective-permute-start(bf16[128,1792]{1,0:T(8,128)(2,1)} %get-tuple-element.16), channel_id=1, source_target_pairs={{0,24},{8,16},{16,8},{24,0},{1,25},{9,17},{17,9},{25,1},{2,26},{10... | collective-permute-start | bytes 1376264 | tf_op jit(solution)/shard_map/ppermute | solution.py:24
  133.2 20.0 %collective-permute-start.17 = (bf16[128,1792]{1,0:T(8,128)(2,1)}, bf16[128,1792]{1,0:T(8,128)(2,1)S(1)}, u32[]{:S(2)}, u32[]{:S(2)}) collective-permute-start(bf16[128,1792]{1,0:T(8,128)(2,1)} %get-tuple-element.16), channel_id=1, source_target_pairs={{0,16},{8,24},{16,0},{24,8},{1,17},{9,25},{17,1},{25,9},{2,18},{10... | collective-permute-start | bytes 1376264 | tf_op jit(solution)/shard_map/ppermute | solution.py:24
  134.8 19.3 %collective-permute-start.16 = (bf16[128,1792]{1,0:T(8,128)(2,1)}, bf16[128,1792]{1,0:T(8,128)(2,1)}, u32[]{:S(2)}, u32[]{:S(2)}) collective-permute-start(bf16[128,1792]{1,0:T(8,128)(2,1)} %get-tuple-element.16), channel_id=1, source_target_pairs={{0,8},{8,0},{16,24},{24,16},{1,9},{9,1},{17,25},{25,17},{2,10},{10... | collective-permute-start | bytes 1376264 | tf_op jit(solution)/shard_map/ppermute | solution.py:24
  159.3 16.4 %collective-permute-start.26 = (f32[512,16]{0,1:T(8,128)S(1)}, f32[512,16]{0,1:T(8,128)S(1)}, u32[]{:S(2)}, u32[]{:S(2)}) collective-permute-start(f32[512,16]{0,1:T(8,128)S(1)} %fusion.1), channel_id=1, source_target_pairs={{0,1},{1,0},{2,3},{3,2},{4,5},{5,4},{6,7},{7,6},{8,9},{9,8},{10,11... | collective-permute-start | bytes 98312 | tf_op jit(solution)/shard_map/ppermute | solution.py:24
  161.4 26.5 %collective-permute-start.36 = (bf16[128,1792]{1,0:T(8,128)(2,1)}, bf16[128,1792]{1,0:T(8,128)(2,1)}, u32[]{:S(2)}, u32[]{:S(2)}) collective-permute-start(bf16[128,1792]{1,0:T(8,128)(2,1)} %pad_maximum_fusion.7), channel_id=1, source_target_pairs={{0,24},{8,16},{16,8},{24,0},{1,25},{9,17},{17,9},{25,1},{2,26},{10... | collective-permute-start | bytes 1376264 | tf_op jit(solution)/shard_map/ppermute | solution.py:24
  164.7 23.6 %collective-permute-start.37 = (bf16[128,1792]{1,0:T(8,128)(2,1)}, bf16[128,1792]{1,0:T(8,128)(2,1)}, u32[]{:S(2)}, u32[]{:S(2)}) collective-permute-start(bf16[128,1792]{1,0:T(8,128)(2,1)} %pad_maximum_fusion.8), channel_id=1, source_target_pairs={{0,16},{8,24},{16,0},{24,8},{1,17},{9,25},{17,1},{25,9},{2,18},{10... | collective-permute-start | bytes 1376264 | tf_op jit(solution)/shard_map/ppermute | solution.py:24
  167.2 21.2 %collective-permute-start.38 = (bf16[128,1792]{1,0:T(8,128)(2,1)}, bf16[128,1792]{1,0:T(8,128)(2,1)}, u32[]{:S(2)}, u32[]{:S(2)}) collective-permute-start(bf16[128,1792]{1,0:T(8,128)(2,1)} %pad_maximum_fusion.9), channel_id=1, source_target_pairs={{0,8},{8,0},{16,24},{24,16},{1,9},{9,1},{17,25},{25,17},{2,10},{10... | collective-permute-start | bytes 1376264 | tf_op jit(solution)/shard_map/ppermute | solution.py:24
  178.0 18.5 %collective-permute-start.19 = (bf16[64,2048]{1,0:T(8,128)(2,1)}, bf16[64,2048]{1,0:T(8,128)(2,1)}, u32[]{:S(2)}, u32[]{:S(2)}) collective-permute-start(bf16[64,2048]{1,0:T(8,128)(2,1)} %get-tuple-element.21), channel_id=1, source_target_pairs={{0,1},{1,0},{2,3},{3,2},{4,5},{5,4},{6,7},{7,6},{8,9},{9,8},{10,11... | collective-permute-start | bytes 786440 | tf_op jit(solution)/shard_map/ppermute | solution.py:24
  184.6 41.7 %collective-permute-start.25 = (bf16[64,2048]{1,0:T(8,128)(2,1)}, bf16[64,2048]{1,0:T(8,128)(2,1)}, u32[]{:S(2)}, u32[]{:S(2)}) collective-permute-start(bf16[64,2048]{1,0:T(8,128)(2,1)} %get-tuple-element.22), channel_id=1, source_target_pairs={{0,1},{1,0},{2,3},{3,2},{4,5},{5,4},{6,7},{7,6},{8,9},{9,8},{10,11... | collective-permute-start | bytes 786440 | tf_op jit(solution)/shard_map/ppermute | solution.py:24
  198.9 28.1 %collective-permute-start.20 = (bf16[64,2048]{1,0:T(8,128)(2,1)}, bf16[64,2048]{1,0:T(8,128)(2,1)}, u32[]{:S(2)}, u32[]{:S(2)}) collective-permute-start(bf16[64,2048]{1,0:T(8,128)(2,1)} %get-tuple-element.18), channel_id=1, source_target_pairs={{0,6},{1,7},{2,4},{3,5},{4,2},{5,3},{6,0},{7,1},{8,14},{9,15},{10,... | collective-permute-start | bytes 786440 | tf_op jit(solution)/shard_map/ppermute | solution.py:24
  219.5 11.7 %collective-permute-start.24 = (bf16[64,2048]{1,0:T(8,128)(2,1)}, bf16[64,2048]{1,0:T(8,128)(2,1)}, u32[]{:S(2)}, u32[]{:S(2)}) collective-permute-start(bf16[64,2048]{1,0:T(8,128)(2,1)} %get-tuple-element.19), channel_id=1, source_target_pairs={{0,2},{1,3},{2,0},{3,1},{4,6},{5,7},{6,4},{7,5},{8,10},{9,11},{10,... | collective-permute-start | bytes 786440 | tf_op jit(solution)/shard_map/ppermute | solution.py:24
  220.2 13.0 %collective-permute-start.22 = (bf16[64,2048]{1,0:T(8,128)(2,1)}, bf16[64,2048]{1,0:T(8,128)(2,1)}, u32[]{:S(2)}, u32[]{:S(2)}) collective-permute-start(bf16[64,2048]{1,0:T(8,128)(2,1)} %get-tuple-element.20), channel_id=1, source_target_pairs={{0,4},{1,5},{2,6},{3,7},{4,0},{5,1},{6,2},{7,3},{8,12},{9,13},{10,... | collective-permute-start | bytes 786440 | tf_op jit(solution)/shard_map/ppermute | solution.py:24
  221.7 14.7 %collective-permute-start.49 = (bf16[64,1792]{1,0:T(8,128)(2,1)}, bf16[64,1792]{1,0:T(8,128)(2,1)}, u32[]{:S(2)}, u32[]{:S(2)}) collective-permute-start(bf16[64,1792]{1,0:T(8,128)(2,1)} %fusion.24), channel_id=1, source_target_pairs={{0,24},{8,16},{16,8},{24,0},{1,25},{9,17},{17,9},{25,1},{2,26},{10... | collective-permute-start | bytes 688136 | tf_op jit(solution)/shard_map/ppermute | solution.py:24
  226.3 10.1 %collective-permute-start.48 = (bf16[64,1792]{1,0:T(8,128)(2,1)}, bf16[64,1792]{1,0:T(8,128)(2,1)S(1)}, u32[]{:S(2)}, u32[]{:S(2)}) collective-permute-start(bf16[64,1792]{1,0:T(8,128)(2,1)} %fusion.24), channel_id=1, source_target_pairs={{0,16},{8,24},{16,0},{24,8},{1,17},{9,25},{17,1},{25,9},{2,18},{10... | collective-permute-start | bytes 688136 | tf_op jit(solution)/shard_map/ppermute | solution.py:24
  (48 other events, 441.6 us)

commit v3 on v2

--- a/solution.py
+++ b/solution.py
@@ -53,16 +53,31 @@
     return jnp.concatenate([block for own in far for block in (own, flip(own, "tensor", 1))])
 
 
-def scatter_dp(x):
+def with_mates_at_once(far):
+    count = far[0].shape[0]
+    mates = flip(jnp.concatenate(far), "tensor", 1)
+    pieces = []
+    for i, own in enumerate(far):
+        pieces += [own, mates[i * count : (i + 1) * count]]
+    return jnp.concatenate(pieces)
+
+
+def scatter_dp(*parts):
     n = lax.axis_size("dp")
     me = lax.axis_index("dp")
     mine = lax.axis_index("tensor")
     size = lax.axis_size("tensor")
     per = size // n
-    count = x.shape[0] // size
+    count = parts[0].shape[0] // size
 
     def group(g):
-        return jnp.concatenate([rows(x, (g * per + i) ^ mine, count) for i in range(per)])
+        return jnp.concatenate(
+            [
+                jnp.concatenate([rows(x, (g * per + i) ^ mine, count) for i in range(per)])
+                for x in parts
+            ],
+            axis=1,
+        )
 
     got = [flip(group(me ^ b), "dp", b) for b in range(n - 1, 0, -1)]
     total = group(me).astype(jnp.float32)
@@ -82,8 +97,10 @@
         return rows(x, ((a // per) ^ other) * per + a % per, count)
 
     total = None
-    for b in range(n - 2, -1, -2):
-        mate = flip(block(me ^ b ^ 1), "tensor", 1).astype(jnp.float32)
+    far = range(n - 2, -1, -2)
+    mates = flip(jnp.concatenate([block(me ^ b ^ 1) for b in far]), "tensor", 1)
+    for i, b in enumerate(far):
+        mate = mates[i * count : (i + 1) * count].astype(jnp.float32)
         pair = block(me ^ b).astype(jnp.float32) + mate
         if b:
             pair = flip(pair.astype(x.dtype), "tensor", b).astype(jnp.float32)
@@ -184,7 +201,7 @@
     far_tokens = far_blocks(tokens, "tensor", 2)
     all_inputs = with_mates(far_tokens)
     far_cot = far_blocks(after(cotangent, *far_tokens), "tensor", 2)
-    all_cot = with_mates(far_cot)
+    all_cot = with_mates_at_once(far_cot)
 
     gate_sum = scatter_dp(dot(all_inputs, gate_weight).astype(bf16))
     rank_parts = jnp.concatenate(
@@ -194,9 +211,10 @@
         ],
         axis=1,
     ).astype(bf16)
-    ranks = scatter_dp(rank_parts).astype(bf16)
-    gate_rank, up_rank = ranks[:, :rank], ranks[:, rank:]
-    up_sum = scatter_dp(dot(all_inputs, up_weight).astype(bf16))
+    up_sums = scatter_dp(dot(all_inputs, up_weight).astype(bf16), rank_parts)
+    up_sum = up_sums[:, :width_here]
+    gate_rank = up_sums[:, width_here : width_here + rank].astype(bf16)
+    up_rank = up_sums[:, width_here + rank :].astype(bf16)
 
     gate_full = gate_sum + adapter_scale * dot(expand(gate_rank, mask_group), gate_raise)
     up_full = up_sum + adapter_scale * dot(expand(up_rank, mask_group), up_raise)
@@ -205,6 +223,7 @@
     all_hidden = jnp.concatenate(far_hidden)
 
     down_back = adapter_scale * collapse(dot(all_cot, down_raise, 1, 1), mask_near)
+    down_back = after(down_back, *far_hidden)
     down_back = reorder(sum_all(down_back, "dp"), "tensor").astype(bf16)
     group_down_back = rows(down_back, dp_index, group_rows)
     down_drop = as_rows(down_in)

time: 242 us -> 246 us (1.017)
  waiting for transfers between devices: 76.6 us -> 81.1 us
    concatenate x12 -> x10, other arithmetic: 10.6 us -> 5.19 us  [group(): jnp.concatenate([rows(x, g * per + i ^ mine, count) for i in range(per)])]
    unnamed x74 -> x58, local copies, waits for them, and re-layouts: 11.2 us -> 16.5 us
    ppermute x50 -> x41, waiting for transfers between devices: 76.6 us -> 81.1 us  [flip(): return lax.ppermute(x, axis, [(i, i ^ bits) for i in range(n)])]
    dynamic_slice x4, local copies, waits for them, and re-layouts: 5.49 us -> 1.97 us  [rows(): return lax.dynamic_slice_in_dim(x, index * count, count)]
    concatenate x0 -> x5, other arithmetic: none -> 3.46 us  [the longest x1 2.28 us: with_mates_at_once(): mates = flip(jnp.concatenate(far), 'tensor', 1)]
    ppermute x50 -> x41, starting transfers between devices: 46.5 us -> 47.1 us  [flip(): return lax.ppermute(x, axis, [(i, i ^ bits) for i in range(n)])]
  transfers between devices with their start and end apart: 50 -> 41, of which waited for: 15 -> 17; matrix products, arithmetic and copies ran while one was open for 41% -> 45% of each run, Pallas kernels for 0% -> 0%
where the time goes in v3:
time: 246 us; the launch traced here: 245 us
  waiting for transfers between devices  81.1 us (33%)
  matrix products  68.2 us (28%)
  starting transfers between devices  47.1 us (19%)
  local copies, waits for them, and re-layouts  24.7 us (10%)
  other arithmetic  22.2 us (9%)
    ppermute x41, waiting for transfers between devices, flip(): return lax.ppermute(x, axis, [(i, i ^ bits) for i in range(n)])  81.1 us
    dot_general x25, matrix products, dot(): lax.dot_general(a, b, (((ca,), (cb,)), ((), ())), preferred_element_type=...  68.2 us
    ppermute x41, starting transfers between devices, flip(): return lax.ppermute(x, axis, [(i, i ^ bits) for i in range(n)])  47.1 us
    unnamed x58, local copies, waits for them, and re-layouts  16.5 us
    concatenate x10, other arithmetic, group(): jnp.concatenate([rows(x, g * per + i ^ mine, count) for i in range(per)])  5.19 us
  transfers between devices with their start and end apart: 41, of which 17 were waited for; matrix products, arithmetic and copies ran while one was open for 45% of the time, Pallas kernels for 0%

profile of v3, /device:TPU:0, one launch (start us, length us, event | category | flops | bytes accessed | tf_op | source)
XLA Modules:
  0.0 244.6 jit_solution(11146910235214022272)
XLA Ops:
  0.6 5.1 %collective-permute-start.5 = (bf16[64,2048]{1,0:T(8,128)(2,1)}, bf16[64,2048]{1,0:T(8,128)(2,1)S(1)}, u32[]{:S(2)}, u32[]{:S(2)}) collective-permute-start(bf16[64,2048]{1,0:T(8,128)(2,1)} %param.13), channel_id=1, source_target_pairs={{0,6},{1,7},{2,4},{3,5},{4,2},{5,3},{6,0},{7,1},{8,14},{9,15},{10,... | collective-permute-start | bytes 786440 | tf_op jit(solution)/shard_map/ppermute | solution.py:24
  17.1 11.2 %collective-permute-done.3 = bf16[64,2048]{1,0:T(8,128)(2,1)} collective-permute-done((bf16[64,2048]{1,0:T(8,128)(2,1)}, bf16[64,2048]{1,0:T(8,128)(2,1)}, u32[]{:S(2)}, u32[]{:S(2)}) %collective-permute-start.3) | collective-permute-done | bytes 262176 | tf_op jit(solution)/shard_map/ppermute | solution.py:24
  28.4 2.5 %collective-permute-start.25 = (bf16[64,2048]{1,0:T(8,128)(2,1)}, bf16[64,2048]{1,0:T(8,128)(2,1)}, u32[]{:S(2)}, u32[]{:S(2)}) collective-permute-start(bf16[64,2048]{1,0:T(8,128)(2,1)} %param.14), channel_id=1, source_target_pairs={{0,6},{1,7},{2,4},{3,5},{4,2},{5,3},{6,0},{7,1},{8,14},{9,15},{10,... | collective-permute-start | bytes 786440 | tf_op jit(solution)/shard_map/ppermute | solution.py:24
  34.5 2.2 fusion.18
  36.7 2.2 fusion.19
  39.9 7.0 %convolution_convert_fusion.2 = bf16[512,1792]{1,0:T(8,128)(2,1)S(1)} fusion(bf16[512,2048]{1,0:T(8,128)(2,1)S(1)} %constant_dynamic-update-slice_fusion, bf16[2048,1792]{1,0:T(8,128)(2,1)} %param.16), kind=kOutput, calls=%fused_computation.2 | convolution fusion | flops 3759013888 | bytes 11272192 | tf_op jit(solution)/shard_map/dot_general | solution.py:13
  47.2 2.5 %collective-permute-start.10 = (bf16[128,1824]{1,0:T(8,128)(2,1)S(1)}, bf16[128,1824]{1,0:T(8,128)(2,1)S(1)}, u32[]{:S(2)}, u32[]{:S(2)}) collective-permute-start(bf16[128,1824]{1,0:T(8,128)(2,1)S(1)} %pad_maximum_fusion.3), channel_id=1, source_target_pairs={{0,24},{8,16},{16,8},{24,0},{1,25},{9,17},{17,9},{25,1},{2,26},{10... | collective-permute-start | bytes 1400840 | tf_op jit(solution)/shard_map/ppermute | solution.py:24
  51.0 7.0 %convolution_convert_fusion.3 = bf16[512,1792]{1,0:T(8,128)(2,1)S(1)} fusion(bf16[512,2048]{1,0:T(8,128)(2,1)S(1)} %constant_dynamic-update-slice_fusion, bf16[2048,1792]{1,0:T(8,128)(2,1)} %param.15), kind=kOutput, calls=%fused_computation.3 | convolution fusion | flops 3759013888 | bytes 11272192 | tf_op jit(solution)/shard_map/dot_general | solution.py:13
  62.2 2.4 collective-permute-start.7
  64.7 8.0 %collective-permute-done.11 = bf16[128,1824]{1,0:T(8,128)(2,1)S(1)} collective-permute-done((bf16[128,1824]{1,0:T(8,128)(2,1)S(1)}, bf16[128,1824]{1,0:T(8,128)(2,1)S(1)}, u32[]{:S(2)}, u32[]{:S(2)}) %collective-permute-start.11) | collective-permute-done | bytes 466976 | tf_op jit(solution)/shard_map/ppermute | solution.py:24
  76.1 2.9 %slice_add_fusion = f32[128,1792]{1,0:T(8,128)} fusion(f32[128,1824]{1,0:T(8,128)} %get-tuple-element.21, bf16[256,1792]{1,0:T(8,128)(2,1)} %bitcast.58, s32[256]{0:T(256)S(1)} %get-tuple-element.127, s32[256]{0:T(256)S(1)} %get-tuple-element.130, s32[128]{0:T(128)S(1)} %eq.326, pred[256]{0:T(512)(128)(4,1)S(1)} %get-tuple-element.124, ...), kind=kOutput, calls=%fused_computation.53 | convolution fusion | flops 119087104 | bytes 2790400 | tf_op jit(solution)/shard_map/dot_general | solution.py:13
  79.0 3.7 %collective-permute-done.7 = bf16[128,1792]{1,0:T(8,128)(2,1)} collective-permute-done((bf16[128,1792]{1,0:T(8,128)(2,1)}, bf16[128,1792]{1,0:T(8,128)(2,1)}, u32[]{:S(2)}, u32[]{:S(2)}) %collective-permute-start.7) | collective-permute-done | bytes 458784 | tf_op jit(solution)/shard_map/ppermute | solution.py:24
  84.6 7.5 %collective-permute-done.8 = bf16[128,1792]{1,0:T(8,128)(2,1)} collective-permute-done((bf16[128,1792]{1,0:T(8,128)(2,1)}, bf16[128,1792]{1,0:T(8,128)(2,1)}, u32[]{:S(2)}, u32[]{:S(2)}) %collective-permute-start.8) | collective-permute-done | bytes 458784 | tf_op jit(solution)/shard_map/ppermute | solution.py:24
  92.2 3.7 %multiply_convert_fusion.2 = (bf16[128,1792]{1,0:T(8,128)(2,1)}, f32[128,1792]{1,0:T(8,128)}) fusion(f32[128,1792]{1,0:T(8,128)} %slice_add_fusion, bf16[128,1792]{1,0:T(8,128)(2,1)} %collective-permute-done.9, bf16[128,1792]{1,0:T(8,128)(2,1)} %collective-permute-done.8, bf16[128,1792]{1,0:T(8,128)(2,1)} %collective-permute-done.7, ...), kind=kOutput, calls=%fused_computation.58 | convolution fusion | flops 122757120 | bytes 5084160 | tf_op jit(solution)/shard_map/dot_general | solution.py:13
  95.9 2.4 collective-permute-start.15
  100.2 2.3 pad_maximum_fusion.2
  102.5 8.0 %collective-permute-done.15 = bf16[128,1792]{1,0:T(8,128)(2,1)S(1)} collective-permute-done((bf16[128,1792]{1,0:T(8,128)(2,1)}, bf16[128,1792]{1,0:T(8,128)(2,1)S(1)}, u32[]{:S(2)}, u32[]{:S(2)}) %collective-permute-start.15) | collective-permute-done | bytes 458784 | tf_op jit(solution)/shard_map/ppermute | solution.py:24
  110.5 8.7 %collective-permute-done.14 = bf16[128,1792]{1,0:T(8,128)(2,1)S(1)} collective-permute-done((bf16[128,1792]{1,0:T(8,128)(2,1)}, bf16[128,1792]{1,0:T(8,128)(2,1)S(1)}, u32[]{:S(2)}, u32[]{:S(2)}) %collective-permute-start.14) | collective-permute-done | bytes 458784 | tf_op jit(solution)/shard_map/ppermute | solution.py:24
  120.8 2.6 %fusion.1 = f32[512,16]{0,1:T(8,128)S(1)} fusion(bf16[256,1792]{1,0:T(8,128)(2,1)} %bitcast.62, s32[512]{0:T(512)S(1)} %eq.346, s32[256]{0:T(256)S(1)} %get-tuple-element.127, s32[256]{0:T(256)S(1)} %get-tuple-element.130, pred[256]{0:T(512)(128)(4,1)S(1)} %get-tuple-element.124, s32[256]{0:T(256)S(1)} %get-tuple-element.128, ...), kind=kOutput, calls=%fused_computation.14 | convolution fusion | flops 481828864 | bytes 2791936 | tf_op jit(solution)/shard_map/dot_general | solution.py:13
  123.4 7.6 %convolution_convert_fusion.1 = bf16[512,2048]{1,0:T(8,128)(2,1)S(1)} fusion(bf16[1792,2048]{1,0:T(8,128)(2,1)} %param.17, bf16[128,1792]{1,0:T(8,128)(2,1)} %copy-done.12, bf16[128,1792]{1,0:T(8,128)(2,1)} %copy-done.13, bf16[128,1792]{1,0:T(8,128)(2,1)} %copy-done.14, bf16[128,1792]{1,0:T(8,128)(2,1)} %get-tuple-element.18), kind=kOutput, calls=%fused_computation.1 | convolution fusion | flops 3766484992 | bytes 11272192 | tf_op jit(solution)/shard_map/dot_general | solution.py:13
  135.1 2.9 %collective-permute-start.22 = (f32[512,16]{0,1:T(8,128)S(1)}, f32[512,16]{0,1:T(8,128)S(1)}, u32[]{:S(2)}, u32[]{:S(2)}) collective-permute-start(f32[512,16]{0,1:T(8,128)S(1)} %add.484), channel_id=1, source_target_pairs={{0,4},{1,5},{2,6},{3,7},{4,0},{5,1},{6,2},{7,3},{8,12},{9,13},{10,... | collective-permute-start | bytes 98312 | tf_op jit(solution)/shard_map/ppermute | solution.py:24
  151.9 7.9 %convolution_convert_fusion = bf16[512,1792]{1,0:T(8,128)(2,1)S(1)} fusion(bf16[512,2048]{1,0:T(8,128)(2,1)} %slice_dynamic-update-slice_fusion, bf16[1792,2048]{1,0:T(8,128)(2,1)} %param.17), kind=kOutput, calls=%fused_computation | convolution fusion | flops 3759013888 | bytes 11272192 | tf_op jit(solution)/shard_map/dot_general | solution.py:13
  170.1 2.9 %convolution_multiply_fusion.3 = f32[32,2048]{1,0:T(8,128)} fusion(bf16[512,2048]{1,0:T(8,128)(2,1)} %slice_dynamic-update-slice_fusion, s32[]{:T(128)S(6)} %mul.255, s32[32]{0:T(128)S(1)} %get-tuple-element.131, s32[32]{0:T(128)S(1)} %get-tuple-element.134, s32[512]{0:T(512)S(1)} %eq.333, pred[32]{0:T(512)(128)(4,1)S(1)} %get-tuple-element.122, ...), kind=kOutput, calls=%fused_computation.7 | convolution fusion | flops 67822592 | bytes 2394693 | tf_op jit(solution)/shard_map/dot_general | solution.py:13
  173.0 14.5 %collective-permute-done.31 = f32[512,16]{0,1:T(8,128)S(1)} collective-permute-done((f32[512,16]{0,1:T(8,128)S(1)}, f32[512,16]{0,1:T(8,128)S(1)}, u32[]{:S(2)}, u32[]{:S(2)}) %collective-permute-start.31) | collective-permute-done | bytes 32800 | tf_op jit(solution)/shard_map/ppermute | solution.py:24
  187.8 3.1 %add_add_fusion = f32[128,1792]{1,0:T(8,128)} fusion(bf16[128,1792]{1,0:T(8,128)(2,1)} %collective-permute-done.29, bf16[128,1792]{1,0:T(8,128)(2,1)} %collective-permute-done.28, bf16[128,1792]{1,0:T(8,128)(2,1)} %collective-permute-done.27, bf16[64,1792]{1,0:T(8,128)(2,1)} %get-tuple-element.38, bf16[64,1792]{1,0:T(8,128)(2,1)S(1)} %get-tuple-element.31, ...), kind=kOutput, calls=%fused_computation.57 | convolution fusion | flops 121151488 | bytes 3679748 | tf_op jit(solution)/shard_map/dot_general | solution.py:13
  190.9 2.3 multiply_convert_fusion.1
  195.0 2.8 %fusion.10 = f32[64,1792]{1,0:T(8,128)} fusion(s32[]{:T(128)S(6)} %mul.269, s32[64]{0:T(128)S(1)} %copy-done.18, s32[64]{0:T(128)S(1)} %copy-done.17, s32[512]{0:T(512)S(1)} %eq.373, pred[64]{0:T(512)(128)(4,1)S(1)} %copy-done.21, bf16[512,16]{0,1:T(8,128)(2,1)S(1)} %maximum_select_fusion.12, bf16[256,16]{0,1:T(8,128)(2,1)S(1)} %get-tuple-element.80, ...), kind=kOutput, calls=%fused_computation.29 | convolution fusion | flops 126035968 | bytes 2329733 | tf_op jit(solution)/shard_map/dot_general | solution.py:13
  203.4 2.1 fusion.22
  224.0 2.4 fusion.25
  226.4 2.4 fusion.26
  232.3 9.5 %collective-permute-done.18 = bf16[64,2048]{1,0:T(8,128)(2,1)S(1)} collective-permute-done((bf16[64,2048]{1,0:T(8,128)(2,1)S(1)}, bf16[64,2048]{1,0:T(8,128)(2,1)S(1)}, u32[]{:S(2)}, u32[]{:S(2)}) %collective-permute-start.18) | collective-permute-done | bytes 262176 | tf_op jit(solution)/shard_map/ppermute | solution.py:24
  241.7 2.9 %add_convert_fusion = bf16[64,2048]{1,0:T(8,128)(2,1)} fusion(bf16[64,2048]{1,0:T(8,128)(2,1)S(1)} %collective-permute-done.19, bf16[64,2048]{1,0:T(8,128)(2,1)S(1)} %collective-permute-done.18, bf16[64,2048]{1,0:T(8,128)(2,1)S(1)} %collective-permute-done.17, bf16[256,2048]{1,0:T(8,128)(2,1)} %collective-permute-done.16, bf16[512,2048]{1,0:T(8,128)(2,1)} %copy-done.5, ...), kind=kOutput, calls=%fused_computation.63 | convolution fusion | flops 69279744 | bytes 2630668 | tf_op jit(solution)/shard_map/dot_general | solution.py:13
  (240 shorter events, 88.1 us)
Async XLA Ops:
  0.6 16.5 %collective-permute-start.5 = (bf16[64,2048]{1,0:T(8,128)(2,1)}, bf16[64,2048]{1,0:T(8,128)(2,1)S(1)}, u32[]{:S(2)}, u32[]{:S(2)}) collective-permute-start(bf16[64,2048]{1,0:T(8,128)(2,1)} %param.13), channel_id=1, source_target_pairs={{0,6},{1,7},{2,4},{3,5},{4,2},{5,3},{6,0},{7,1},{8,14},{9,15},{10,... | collective-permute-start | bytes 786440 | tf_op jit(solution)/shard_map/ppermute | solution.py:24
  5.8 22.6 %collective-permute-start.3 = (bf16[64,2048]{1,0:T(8,128)(2,1)}, bf16[64,2048]{1,0:T(8,128)(2,1)}, u32[]{:S(2)}, u32[]{:S(2)}) collective-permute-start(bf16[64,2048]{1,0:T(8,128)(2,1)} %param.13), channel_id=1, source_target_pairs={{0,4},{1,5},{2,6},{3,7},{4,0},{5,1},{6,2},{7,3},{8,12},{9,13},{10,... | collective-permute-start | bytes 786440 | tf_op jit(solution)/shard_map/ppermute | solution.py:24
  5.8 22.6 %collective-permute-start.1 = (bf16[64,2048]{1,0:T(8,128)(2,1)}, bf16[64,2048]{1,0:T(8,128)(2,1)}, u32[]{:S(2)}, u32[]{:S(2)}) collective-permute-start(bf16[64,2048]{1,0:T(8,128)(2,1)} %param.13), channel_id=1, source_target_pairs={{0,2},{1,3},{2,0},{3,1},{4,6},{5,7},{6,4},{7,5},{8,10},{9,11},{10,... | collective-permute-start | bytes 786440 | tf_op jit(solution)/shard_map/ppermute | solution.py:24
  6.4 25.0 %collective-permute-start = (bf16[64,2048]{1,0:T(8,128)(2,1)}, bf16[64,2048]{1,0:T(8,128)(2,1)}, u32[]{:S(2)}, u32[]{:S(2)}) collective-permute-start(bf16[64,2048]{1,0:T(8,128)(2,1)} %param.13), channel_id=1, source_target_pairs={{0,1},{1,0},{2,3},{3,2},{4,5},{5,4},{6,7},{7,6},{8,9},{9,8},{10,11... | collective-permute-start | bytes 786440 | tf_op jit(solution)/shard_map/ppermute | solution.py:24
  28.4 70.5 %collective-permute-start.25 = (bf16[64,2048]{1,0:T(8,128)(2,1)}, bf16[64,2048]{1,0:T(8,128)(2,1)}, u32[]{:S(2)}, u32[]{:S(2)}) collective-permute-start(bf16[64,2048]{1,0:T(8,128)(2,1)} %param.14), channel_id=1, source_target_pairs={{0,6},{1,7},{2,4},{3,5},{4,2},{5,3},{6,0},{7,1},{8,14},{9,15},{10,... | collective-permute-start | bytes 786440 | tf_op jit(solution)/shard_map/ppermute | solution.py:24
  30.9 69.3 %collective-permute-start.24 = (bf16[64,2048]{1,0:T(8,128)(2,1)}, bf16[64,2048]{1,0:T(8,128)(2,1)}, u32[]{:S(2)}, u32[]{:S(2)}) collective-permute-start(bf16[64,2048]{1,0:T(8,128)(2,1)} %param.14), channel_id=1, source_target_pairs={{0,4},{1,5},{2,6},{3,7},{4,0},{5,1},{6,2},{7,3},{8,12},{9,13},{10,... | collective-permute-start | bytes 786440 | tf_op jit(solution)/shard_map/ppermute | solution.py:24
  47.2 15.0 %collective-permute-start.10 = (bf16[128,1824]{1,0:T(8,128)(2,1)S(1)}, bf16[128,1824]{1,0:T(8,128)(2,1)S(1)}, u32[]{:S(2)}, u32[]{:S(2)}) collective-permute-start(bf16[128,1824]{1,0:T(8,128)(2,1)S(1)} %pad_maximum_fusion.3), channel_id=1, source_target_pairs={{0,24},{8,16},{16,8},{24,0},{1,25},{9,17},{17,9},{25,1},{2,26},{10... | collective-permute-start | bytes 1400840 | tf_op jit(solution)/shard_map/ppermute | solution.py:24
  49.7 22.9 %collective-permute-start.11 = (bf16[128,1824]{1,0:T(8,128)(2,1)S(1)}, bf16[128,1824]{1,0:T(8,128)(2,1)S(1)}, u32[]{:S(2)}, u32[]{:S(2)}) collective-permute-start(bf16[128,1824]{1,0:T(8,128)(2,1)S(1)} %pad_maximum_fusion.4), channel_id=1, source_target_pairs={{0,16},{8,24},{16,0},{24,8},{1,17},{9,25},{17,1},{25,9},{2,18},{10... | collective-permute-start | bytes 1400840 | tf_op jit(solution)/shard_map/ppermute | solution.py:24
  50.4 23.8 %collective-permute-start.12 = (bf16[128,1824]{1,0:T(8,128)(2,1)S(1)}, bf16[128,1824]{1,0:T(8,128)(2,1)S(1)}, u32[]{:S(2)}, u32[]{:S(2)}) collective-permute-start(bf16[128,1824]{1,0:T(8,128)(2,1)S(1)} %pad_maximum_fusion.5), channel_id=1, source_target_pairs={{0,8},{8,0},{16,24},{24,16},{1,9},{9,1},{17,25},{25,17},{2,10},{10... | collective-permute-start | bytes 1400840 | tf_op jit(solution)/shard_map/ppermute | solution.py:24
  62.2 20.5 %collective-permute-start.7 = (bf16[128,1792]{1,0:T(8,128)(2,1)}, bf16[128,1792]{1,0:T(8,128)(2,1)}, u32[]{:S(2)}, u32[]{:S(2)}) collective-permute-start(bf16[128,1792]{1,0:T(8,128)(2,1)} %pad_maximum_fusion.6), channel_id=1, source_target_pairs={{0,24},{8,16},{16,8},{24,0},{1,25},{9,17},{17,9},{25,1},{2,26},{10... | collective-permute-start | bytes 1376264 | tf_op jit(solution)/shard_map/ppermute | solution.py:24
  72.7 19.4 %collective-permute-start.8 = (bf16[128,1792]{1,0:T(8,128)(2,1)}, bf16[128,1792]{1,0:T(8,128)(2,1)}, u32[]{:S(2)}, u32[]{:S(2)}) collective-permute-start(bf16[128,1792]{1,0:T(8,128)(2,1)} %pad_maximum_fusion.7), channel_id=1, source_target_pairs={{0,16},{8,24},{16,0},{24,8},{1,17},{9,25},{17,1},{25,9},{2,18},{10... | collective-permute-start | bytes 1376264 | tf_op jit(solution)/shard_map/ppermute | solution.py:24
  74.2 18.0 %collective-permute-start.9 = (bf16[128,1792]{1,0:T(8,128)(2,1)}, bf16[128,1792]{1,0:T(8,128)(2,1)}, u32[]{:S(2)}, u32[]{:S(2)}) collective-permute-start(bf16[128,1792]{1,0:T(8,128)(2,1)} %pad_maximum_fusion.8), channel_id=1, source_target_pairs={{0,8},{8,0},{16,24},{24,16},{1,9},{9,1},{17,25},{25,17},{2,10},{10... | collective-permute-start | bytes 1376264 | tf_op jit(solution)/shard_map/ppermute | solution.py:24
  82.7 17.4 %collective-permute-start.23 = (bf16[64,2048]{1,0:T(8,128)(2,1)S(1)}, bf16[64,2048]{1,0:T(8,128)(2,1)}, u32[]{:S(2)}, u32[]{:S(2)}) collective-permute-start(bf16[64,2048]{1,0:T(8,128)(2,1)S(1)} %copy-done.6), channel_id=1, source_target_pairs={{0,2},{1,3},{2,0},{3,1},{4,6},{5,7},{6,4},{7,5},{8,10},{9,11},{10,... | collective-permute-start | bytes 786440 | tf_op jit(solution)/shard_map/ppermute | solution.py:24
  95.9 14.5 %collective-permute-start.15 = (bf16[128,1792]{1,0:T(8,128)(2,1)}, bf16[128,1792]{1,0:T(8,128)(2,1)S(1)}, u32[]{:S(2)}, u32[]{:S(2)}) collective-permute-start(bf16[128,1792]{1,0:T(8,128)(2,1)} %get-tuple-element.18), channel_id=1, source_target_pairs={{0,24},{8,16},{16,8},{24,0},{1,25},{9,17},{17,9},{25,1},{2,26},{10... | collective-permute-start | bytes 1376264 | tf_op jit(solution)/shard_map/ppermute | solution.py:24
  98.3 20.9 %collective-permute-start.14 = (bf16[128,1792]{1,0:T(8,128)(2,1)}, bf16[128,1792]{1,0:T(8,128)(2,1)S(1)}, u32[]{:S(2)}, u32[]{:S(2)}) collective-permute-start(bf16[128,1792]{1,0:T(8,128)(2,1)} %get-tuple-element.18), channel_id=1, source_target_pairs={{0,16},{8,24},{16,0},{24,8},{1,17},{9,25},{17,1},{25,9},{2,18},{10... | collective-permute-start | bytes 1376264 | tf_op jit(solution)/shard_map/ppermute | solution.py:24
  98.9 20.4 %collective-permute-start.13 = (bf16[128,1792]{1,0:T(8,128)(2,1)}, bf16[128,1792]{1,0:T(8,128)(2,1)S(1)}, u32[]{:S(2)}, u32[]{:S(2)}) collective-permute-start(bf16[128,1792]{1,0:T(8,128)(2,1)} %get-tuple-element.18), channel_id=1, source_target_pairs={{0,8},{8,0},{16,24},{24,16},{1,9},{9,1},{17,25},{25,17},{2,10},{10... | collective-permute-start | bytes 1376264 | tf_op jit(solution)/shard_map/ppermute | solution.py:24
  102.4 37.8 %collective-permute-start.26 = (bf16[256,2048]{1,0:T(8,128)(2,1)}, bf16[256,2048]{1,0:T(8,128)(2,1)}, u32[]{:S(2)}, u32[]{:S(2)}) collective-permute-start(bf16[256,2048]{1,0:T(8,128)(2,1)} %pad_maximum_fusion.2), channel_id=1, source_target_pairs={{0,1},{1,0},{2,3},{3,2},{4,5},{5,4},{6,7},{7,6},{8,9},{9,8},{10,11... | collective-permute-start | bytes 3145736 | tf_op jit(solution)/shard_map/ppermute | solution.py:24
  123.4 7.7 %collective-permute-start.20 = (f32[512,16]{0,1:T(8,128)S(1)}, f32[512,16]{0,1:T(8,128)S(1)}, u32[]{:S(2)}, u32[]{:S(2)}) collective-permute-start(f32[512,16]{0,1:T(8,128)S(1)} %fusion.1), channel_id=1, source_target_pairs={{0,1},{1,0},{2,3},{3,2},{4,5},{5,4},{6,7},{7,6},{8,9},{9,8},{10,11... | collective-permute-start | bytes 98312 | tf_op jit(solution)/shard_map/ppermute | solution.py:24
  139.1 78.9 %collective-permute-start.16 = (bf16[256,2048]{1,0:T(8,128)(2,1)}, bf16[256,2048]{1,0:T(8,128)(2,1)}, u32[]{:S(2)}, u32[]{:S(2)}) collective-permute-start(bf16[256,2048]{1,0:T(8,128)(2,1)} %pad_maximum_fusion.1), channel_id=1, source_target_pairs={{0,1},{1,0},{2,3},{3,2},{4,5},{5,4},{6,7},{7,6},{8,9},{9,8},{10,11... | collective-permute-start | bytes 3145736 | tf_op jit(solution)/shard_map/ppermute | solution.py:24
  161.8 7.5 %collective-permute-start.30 = (f32[512,16]{0,1:T(8,128)S(1)}, f32[512,16]{0,1:T(8,128)S(1)}, u32[]{:S(2)}, u32[]{:S(2)}) collective-permute-start(f32[512,16]{0,1:T(8,128)S(1)} %convolution_multiply_fusion.4), channel_id=1, source_target_pairs={{0,8},{8,0},{16,24},{24,16},{1,9},{9,1},{17,25},{25,17},{2,10},{10... | collective-permute-start | bytes 98312 | tf_op jit(solution)/shard_map/ppermute | solution.py:24
  164.1 23.7 %collective-permute-start.27 = (bf16[128,1792]{1,0:T(8,128)(2,1)}, bf16[128,1792]{1,0:T(8,128)(2,1)}, u32[]{:S(2)}, u32[]{:S(2)}) collective-permute-start(bf16[128,1792]{1,0:T(8,128)(2,1)} %pad_maximum_fusion.9), channel_id=1, source_target_pairs={{0,24},{8,16},{16,8},{24,0},{1,25},{9,17},{17,9},{25,1},{2,26},{10... | collective-permute-start | bytes 1376264 | tf_op jit(solution)/shard_map/ppermute | solution.py:24
  166.4 21.4 %collective-permute-start.28 = (bf16[128,1792]{1,0:T(8,128)(2,1)}, bf16[128,1792]{1,0:T(8,128)(2,1)}, u32[]{:S(2)}, u32[]{:S(2)}) collective-permute-start(bf16[128,1792]{1,0:T(8,128)(2,1)} %pad_maximum_fusion.10), channel_id=1, source_target_pairs={{0,16},{8,24},{16,0},{24,8},{1,17},{9,25},{17,1},{25,9},{2,18},{10... | collective-permute-start | bytes 1376264 | tf_op jit(solution)/shard_map/ppermute | solution.py:24
  167.7 20.1 %collective-permute-start.29 = (bf16[128,1792]{1,0:T(8,128)(2,1)}, bf16[128,1792]{1,0:T(8,128)(2,1)}, u32[]{:S(2)}, u32[]{:S(2)}) collective-permute-start(bf16[128,1792]{1,0:T(8,128)(2,1)} %pad_maximum_fusion.11), channel_id=1, source_target_pairs={{0,8},{8,0},{16,24},{24,16},{1,9},{9,1},{17,25},{25,17},{2,10},{10... | collective-permute-start | bytes 1376264 | tf_op jit(solution)/shard_map/ppermute | solution.py:24
  169.2 18.3 %collective-permute-start.31 = (f32[512,16]{0,1:T(8,128)S(1)}, f32[512,16]{0,1:T(8,128)S(1)}, u32[]{:S(2)}, u32[]{:S(2)}) collective-permute-start(f32[512,16]{0,1:T(8,128)S(1)} %add.495), channel_id=1, source_target_pairs={{0,16},{8,24},{16,0},{24,8},{1,17},{9,25},{17,1},{25,9},{2,18},{10... | collective-permute-start | bytes 98312 | tf_op jit(solution)/shard_map/ppermute | solution.py:24
  206.3 6.6 %collective-permute-start.37 = (bf16[128,32]{0,1:T(8,128)(2,1)S(1)}, bf16[128,32]{0,1:T(8,128)(2,1)S(1)}, u32[]{:S(2)}, u32[]{:S(2)}) collective-permute-start(bf16[128,32]{0,1:T(8,128)(2,1)S(1)} %add_convert_fusion.4), channel_id=1, source_target_pairs={{0,16},{8,24},{16,0},{24,8},{1,17},{9,25},{17,1},{25,9},{2,18},{10... | collective-permute-start | bytes 24584 | tf_op jit(solution)/shard_map/ppermute | solution.py:24
  208.3 6.7 %collective-permute-start.35 = (bf16[128,32]{0,1:T(8,128)(2,1)S(1)}, bf16[128,32]{0,1:T(8,128)(2,1)S(1)}, u32[]{:S(2)}, u32[]{:S(2)}) collective-permute-start(bf16[128,32]{0,1:T(8,128)(2,1)S(1)} %add_convert_fusion.4), channel_id=1, source_target_pairs={{0,8},{8,0},{16,24},{24,16},{1,9},{9,1},{17,25},{25,17},{2,10},{10... | collective-permute-start | bytes 24584 | tf_op jit(solution)/shard_map/ppermute | solution.py:24
  211.4 10.5 %collective-permute-start.40 = (bf16[64,1792]{1,0:T(8,128)(2,1)}, bf16[64,1792]{1,0:T(8,128)(2,1)}, u32[]{:S(2)}, u32[]{:S(2)}) collective-permute-start(bf16[64,1792]{1,0:T(8,128)(2,1)} %fusion.24), channel_id=1, source_target_pairs={{0,24},{8,16},{16,8},{24,0},{1,25},{9,17},{17,9},{25,1},{2,26},{10... | collective-permute-start | bytes 688136 | tf_op jit(solution)/shard_map/ppermute | solution.py:24
  212.9 11.1 %collective-permute-start.39 = (bf16[64,1792]{1,0:T(8,128)(2,1)}, bf16[64,1792]{1,0:T(8,128)(2,1)}, u32[]{:S(2)}, u32[]{:S(2)}) collective-permute-start(bf16[64,1792]{1,0:T(8,128)(2,1)} %fusion.24), channel_id=1, source_target_pairs={{0,16},{8,24},{16,0},{24,8},{1,17},{9,25},{17,1},{25,9},{2,18},{10... | collective-permute-start | bytes 688136 | tf_op jit(solution)/shard_map/ppermute | solution.py:24
  213.4 10.6 %collective-permute-start.38 = (bf16[64,1792]{1,0:T(8,128)(2,1)}, bf16[64,1792]{1,0:T(8,128)(2,1)}, u32[]{:S(2)}, u32[]{:S(2)}) collective-permute-start(bf16[64,1792]{1,0:T(8,128)(2,1)} %fusion.24), channel_id=1, source_target_pairs={{0,8},{8,0},{16,24},{24,16},{1,9},{9,1},{17,25},{25,17},{2,10},{10... | collective-permute-start | bytes 688136 | tf_op jit(solution)/shard_map/ppermute | solution.py:24
  219.5 11.2 %collective-permute-start.17 = (bf16[64,2048]{1,0:T(8,128)(2,1)S(1)}, bf16[64,2048]{1,0:T(8,128)(2,1)S(1)}, u32[]{:S(2)}, u32[]{:S(2)}) collective-permute-start(bf16[64,2048]{1,0:T(8,128)(2,1)S(1)} %get-tuple-element.22), channel_id=1, source_target_pairs={{0,6},{1,7},{2,4},{3,5},{4,2},{5,3},{6,0},{7,1},{8,14},{9,15},{10,... | collective-permute-start | bytes 786440 | tf_op jit(solution)/shard_map/ppermute | solution.py:24
  221.5 10.8 %collective-permute-start.19 = (bf16[64,2048]{1,0:T(8,128)(2,1)S(1)}, bf16[64,2048]{1,0:T(8,128)(2,1)S(1)}, u32[]{:S(2)}, u32[]{:S(2)}) collective-permute-start(bf16[64,2048]{1,0:T(8,128)(2,1)S(1)} %get-tuple-element.23), channel_id=1, source_target_pairs={{0,2},{1,3},{2,0},{3,1},{4,6},{5,7},{6,4},{7,5},{8,10},{9,11},{10,... | collective-permute-start | bytes 786440 | tf_op jit(solution)/shard_map/ppermute | solution.py:24
  221.9 19.8 %collective-permute-start.18 = (bf16[64,2048]{1,0:T(8,128)(2,1)S(1)}, bf16[64,2048]{1,0:T(8,128)(2,1)S(1)}, u32[]{:S(2)}, u32[]{:S(2)}) collective-permute-start(bf16[64,2048]{1,0:T(8,128)(2,1)S(1)} %get-tuple-element.24), channel_id=1, source_target_pairs={{0,4},{1,5},{2,6},{3,7},{4,0},{5,1},{6,2},{7,3},{8,12},{9,13},{10,... | collective-permute-start | bytes 786440 | tf_op jit(solution)/shard_map/ppermute | solution.py:24
  (31 other events, 282.1 us)
